TPU v7x, 32 devices: a whole 2x2x4 slice. The times are simulated.
32 devices in a mesh: clus: 8 (over y, x, core), dir: 4 (over z).
Axes of the slice: x: 2, y: 2, z: 4, core: 2. Of those that a mesh axis runs over, the one named last changes fastest.
Arguments:
- sources: bfloat16 [96, 32768], P(None, ('clus', 'dir')), may hold values from -6 to 6
- live_counts: int32 [8, 4], P('clus'), may hold values from 1 to 16, 32 in all within a row
- aggregate: bfloat16 [512, 96], replicated, may hold values from -0.625 to 0.625
- translators: bfloat16 [316, 512], P(None, 'dir'), may hold values from -0.21875 to 0.21875
- boundary_lists: int32 [8, 2, 32], P('clus'), may hold values from 0 to 63
- far_sources: int32 [512, 128], P('clus'), may hold values from 0 to 127
- far_translators: int32 [512, 128], P('clus'), may hold values from 0 to 315
- near_blocks: bfloat16 [512, 96, 576], P(('clus', 'dir')), may hold values from -0.25 to 0.25
- near_columns: int32 [512, 6], P(('clus', 'dir')), may hold values from 0 to 15
Outputs:
- field: bfloat16 [96, 32768], P(None, ('clus', 'dir'))
Inputs may be any that keep to these rules, and one draw needn't show every extreme that they name: `live_counts`: A cluster's counts add to 32; in every cluster some device holds all 16 of its slots. `far_sources`: values below 64 name the cluster's own slots, the next 32 the boxes received from the previous cluster, the last 32 those from the next cluster.
All inputs are finite; a program needn't handle non-finite values.
Results may differ from a plain program's by a relative error of at most 0.0075.
Values may be sent and summed in bfloat16 or wider, within the bound.
A program may use at most 64 MiB of HBM per device.

v0:
```python
import math

import jax
import jax.numpy as jnp
from jax import lax
from jax.sharding import PartitionSpec as P

BOX_DEV = 8


def shifted(value, axis, steps):
    count = lax.axis_size(axis)
    leading, last = (max(0, -steps), min(count, count - steps))
    return lax.ppermute(value, axis, [(source, source + steps) for source in range(leading, last)])


def translate_block(block_lists, kind_table, extended):
    source_ids, kind_ids = block_lists
    kind_count = kind_table.shape[0]
    ext_slots = extended.shape[1]
    pick_kind = (
        kind_ids[:, :, None] == jnp.arange(kind_count, dtype=jnp.int32)[None, None, :]
    ).astype(jnp.bfloat16)
    values = jnp.einsum(
        "tin,nk->tik", pick_kind, kind_table, preferred_element_type=jnp.float32
    ).astype(jnp.bfloat16)
    pick_source = (
        source_ids[:, :, None] == jnp.arange(ext_slots, dtype=jnp.int32)[None, None, :]
    ).astype(jnp.bfloat16)
    weights = jnp.einsum("tis,tik->tks", pick_source, values, preferred_element_type=jnp.float32)
    weight_high = weights.astype(jnp.bfloat16)
    weight_low = (weights - weight_high.astype(jnp.float32)).astype(jnp.bfloat16)
    high_part = jnp.einsum(
        "tks,ksr->ktr", weight_high, extended, preferred_element_type=jnp.float32
    )
    low_part = jnp.einsum("tks,ksr->ktr", weight_low, extended, preferred_element_type=jnp.float32)
    return high_part + low_part


def per_device(
    sources,
    live_counts,
    aggregate,
    translators,
    boundary_lists,
    far_sources,
    far_translators,
    near_blocks,
    near_columns,
):
    dir_count = lax.axis_size("dir")
    dir_index = lax.axis_index("dir")
    unknowns = sources.shape[0]
    capacity = near_blocks.shape[0]
    rights = sources.shape[1] // capacity
    dir_slice = translators.shape[1]
    cluster_slots = far_sources.shape[0]
    interactions = far_sources.shape[1]
    neighbours = near_columns.shape[1]
    counts_here = live_counts[0]
    own_count = lax.dynamic_index_in_dim(counts_here, dir_index, 0, keepdims=False)
    own_live = jnp.arange(capacity, dtype=jnp.int32) < own_count
    local_units = (
        sources.reshape(unknowns, capacity, rights) * own_live.astype(jnp.bfloat16)[None, :, None]
    )
    masked = local_units.reshape(unknowns, capacity * rights)
    stacked = local_units[:, near_columns, :]
    blocks = near_blocks.reshape(capacity, unknowns, neighbours, unknowns)
    near_part = jnp.einsum("sujv,vsjr->usr", blocks, stacked, preferred_element_type=jnp.float32)
    gathered = lax.all_gather(masked, "dir", axis=1, tiled=True)
    upper_end = jnp.cumsum(counts_here)
    lower_end = upper_end - counts_here
    box_total = BOX_DEV * dir_count
    box_ranks = jnp.arange(box_total, dtype=jnp.int32)
    owners = jnp.sum((upper_end[None, :] <= box_ranks[:, None]).astype(jnp.int32), axis=1)
    positions = owners * capacity + box_ranks - lower_end[owners]
    direction_rows = lax.dynamic_slice_in_dim(aggregate, dir_index * dir_slice, dir_slice, 0)
    picked = gathered.reshape(unknowns, cluster_slots, rights)[:, positions, :].reshape(
        unknowns, box_total * rights
    )
    compact = jnp.dot(direction_rows, picked, preferred_element_type=jnp.float32).astype(
        jnp.bfloat16
    )
    relayed = (
        jnp.zeros((dir_slice, cluster_slots, rights), jnp.bfloat16)
        .at[:, positions, :]
        .set(compact.reshape(dir_slice, box_total, rights))
    )
    boundary_here = boundary_lists[0]
    bound_count = boundary_here.shape[1]
    upward = relayed[:, boundary_here[0], :].reshape(dir_slice, bound_count * rights)
    downward = relayed[:, boundary_here[1], :].reshape(dir_slice, bound_count * rights)
    from_before = shifted(upward, "clus", 1)
    from_after = shifted(downward, "clus", -1)
    extended = jnp.concatenate(
        [
            relayed,
            from_before.reshape(dir_slice, bound_count, rights),
            from_after.reshape(dir_slice, bound_count, rights),
        ],
        axis=1,
    )
    block_rows = math.gcd(cluster_slots, 64)
    block_count = cluster_slots // block_rows
    pieces = lax.map(
        lambda block_lists: translate_block(block_lists, translators, extended),
        (
            far_sources.reshape(block_count, block_rows, interactions),
            far_translators.reshape(block_count, block_rows, interactions),
        ),
    )
    incoming = (
        pieces.transpose(1, 0, 2, 3).reshape(dir_slice, cluster_slots * rights).astype(jnp.bfloat16)
    )
    returned = lax.all_to_all(incoming, "dir", split_axis=1, concat_axis=0, tiled=True)
    far_part = jnp.einsum("ku,kc->uc", aggregate, returned, preferred_element_type=jnp.float32)
    summed = (far_part.reshape(unknowns, capacity, rights) + near_part) * own_live.astype(
        jnp.float32
    )[None, :, None]
    return summed.reshape(unknowns, capacity * rights).astype(jnp.bfloat16)


def solution(mesh):
    in_specs = (
        P(None, ("clus", "dir")),
        P("clus", None),
        P(),
        P(None, "dir"),
        P("clus", None, None),
        P("clus", None),
        P("clus", None),
        P(("clus", "dir"), None, None),
        P(("clus", "dir"), None),
    )
    out_specs = P(None, ("clus", "dir"))
    return jax.shard_map(
        per_device, mesh=mesh, in_specs=in_specs, out_specs=out_specs, check_vma=False
    )
```

profile of v0, /device:TPU:1, one launch (start us, length us, event | category | flops | bytes accessed | tf_op | source)
XLA Modules:
  0.0 114.5 jit_solution(11627593804350274630)
XLA Ops:
  0.0 0.9 reduce-window.8
  2.2 2.5 %fusion.19 = s32[32]{0:T(128)S(1)} fusion(s32[32]{0:T(128)S(1)} %convert_reduce_fusion, s32[]{:T(128)} %bitcast.5, s32[]{:T(128)} %bitcast.6, s32[]{:T(128)} %bitcast.8, s32[]{:T(128)} %bitcast.7), kind=kLoop, calls=%fused_computation.45 | loop fusion | flops 480 | bytes 272 | tf_op jit(solution)/shard_map/select_n | solution.py:87
  4.7 1.2 %constant_dynamic-slice_fusion = s32[1,1]{1,0:T(1,128)} fusion(s32[1,4]{1,0:T(1,128)} %param.10, s32[]{:T(128)S(6)} %select_n.54), kind=kLoop, calls=%fused_computation.51 | loop fusion | bytes 12 | tf_op jit(solution)/shard_map/jit(dynamic_index_in_dim)/dynamic_slice | solution.py:61
  6.8 0.9 broadcast_multiply_fusion.1
  7.7 18.0 %all_gather.3 = bf16[96,4096]{1,0:T(8,128)(2,1)S(1)} all-gather(bf16[96,1024]{1,0:T(8,128)(2,1)S(1)} %broadcast_multiply_fusion.1), channel_id=1, replica_groups=mesh['clus'=8,'dir'=4] {'dir'}, dimensions={1}, use_global_device_ids=true | all-gather | bytes 983040 | tf_op jit(solution)/shard_map/all_gather | solution.py:70
  28.0 1.6 %scatter_fusion = bf16[128,64,64]{0,2,1:T(8,128)(2,1)S(1)} fusion(bf16[128,64,64]{0,2,1:T(8,128)(2,1)S(1)} %broadcast_in_dim.10, s32[32]{0:T(128)S(1)} %fusion.19, bf16[32,128,64]{1,2,0:T(8,128)(2,1)S(1)} %bitcast.80), kind=kCustom, calls=%fused_computation.4 | custom fusion | bytes 1572992 | tf_op jit(solution)/shard_map/scatter | solution.py:87
  30.2 6.3 %collective-permute-start = (bf16[128,2048]{0,1:T(8,128)(2,1)S(1)}, bf16[128,2048]{0,1:T(8,128)(2,1)}, u32[]{:S(2)}, u32[]{:S(2)}) collective-permute-start(bf16[128,2048]{0,1:T(8,128)(2,1)S(1)} %bitcast.86), channel_id=1, source_target_pairs={{0,4},{4,8},{8,12},{12,16},{16,20},{20,24},{24,28},{1,5},{5,9},{9,... | collective-permute-start | bytes 1572872 | tf_op jit(solution)/shard_map/ppermute | solution.py:14
  36.6 1.4 %gather_fusion.2 = bf16[32,128,64]{1,2,0:T(8,128)(2,1)} fusion(bf16[128,64,64]{0,2,1:T(8,128)(2,1)S(1)} %scatter_fusion, s32[1024]{0:T(1024)S(1)} %get-tuple-element.33), kind=kCustom, calls=%fused_computation.2 | custom fusion | bytes 1048704 | tf_op jit(solution)/shard_map/gather | solution.py:92
  38.0 2.0 %collective-permute-start.1 = (bf16[128,2048]{0,1:T(8,128)(2,1)}, bf16[128,2048]{0,1:T(8,128)(2,1)}, u32[]{:S(2)}, u32[]{:S(2)}) collective-permute-start(bf16[128,2048]{0,1:T(8,128)(2,1)} %bitcast.24), channel_id=1, source_target_pairs={{4,0},{8,4},{12,8},{16,12},{20,16},{24,20},{28,24},{5,1},{9,5},{13... | collective-permute-start | bytes 1572872 | tf_op jit(solution)/shard_map/ppermute | solution.py:14
  40.1 4.5 %copy.55 = bf16[128,64,64]{1,2,0:T(8,128)(2,1)} copy(bf16[128,64,64]{0,2,1:T(8,128)(2,1)S(1)} %scatter_fusion) | data formatting | bytes 2097152 | tf_op jit(solution)/shard_map/scatter | solution.py:87
  44.6 1.3 %iota_compare_fusion = pred[64,128,316]{1,0,2:T(32,128)(4,1)S(1)} fusion(s32[64,128]{1,0:T(8,128)S(1)} %copy-done.5), kind=kLoop, calls=%fused_computation.7 | loop fusion | flops 2588672 | bytes 2621440 | tf_op jit(solution)/shard_map/while/body/eval_jaxpr/eq | solution.py:22
  45.9 7.8 %subtract_convert_fusion = (bf16[64,128,128]{2,1,0:T(8,128)(2,1)}, bf16[64,128,128]{2,1,0:T(8,128)(2,1)}) fusion(s32[64,128]{1,0:T(8,128)S(1)} %copy-done.9, pred[64,128,316]{1,0,2:T(32,128)(4,1)S(1)} %iota_compare_fusion, bf16[316,128]{1,0:T(8,128)(2,1)S(1)} %copy-done.8), kind=kOutput, calls=%fused_computation.9 | convolution fusion | flops 937426944 | bytes 6896640 | tf_op jit(solution)/shard_map/while/body/eval_jaxpr/tis,tik->tks/dot_general | solution.py:30
  53.7 4.5 %copy.56 = bf16[128,32,64]{1,2,0:T(8,128)(2,1)S(1)} copy(bf16[128,32,64]{0,2,1:T(8,128)(2,1)} %bitcast.20) | data formatting | bytes 1048576 | tf_op jit(solution)/shard_map/reshape | solution.py:98
  58.2 5.3 %copy.57 = bf16[128,32,64]{1,2,0:T(8,128)(2,1)} copy(bf16[128,32,64]{0,2,1:T(8,128)(2,1)} %bitcast.25) | data formatting | bytes 1048576 | tf_op jit(solution)/shard_map/reshape | solution.py:99
  63.5 5.8 %fusion.3 = f32[128,64,64]{2,1,0:T(8,128)S(1)} fusion(bf16[64,128,128]{2,1,0:T(8,128)(2,1)} %get-tuple-element.15, bf16[128,32,64]{1,2,0:T(8,128)(2,1)} %copy.57, bf16[128,32,64]{1,2,0:T(8,128)(2,1)S(1)} %copy.56, bf16[128,64,64]{1,2,0:T(8,128)(2,1)} %copy.55), kind=kOutput, calls=%fused_computation.14 | convolution fusion | flops 140509184 | bytes 6291456 | tf_op jit(solution)/shard_map/while/body/eval_jaxpr/tks,ksr->ktr/dot_general | solution.py:36
  69.3 6.6 %add_convert_fusion = bf16[128,64,64]{2,1,0:T(8,128)(2,1)} fusion(f32[128,64,64]{2,1,0:T(8,128)S(1)} %fusion.3, bf16[64,128,128]{2,1,0:T(8,128)(2,1)S(1)} %copy-done.3, bf16[128,32,64]{1,2,0:T(8,128)(2,1)S(1)} %copy-done.1, bf16[128,32,64]{1,2,0:T(8,128)(2,1)S(1)} %copy.56, bf16[128,64,64]{1,2,0:T(8,128)(2,1)S(1)} %copy-done.2), kind=kOutput, calls=%fused_computation.8 | convolution fusion | flops 141557760 | bytes 7340032 | tf_op jit(solution)/shard_map/while/body/eval_jaxpr/tks,ksr->ktr/dot_general | solution.py:33
  75.9 4.1 %copy.60 = bf16[128,64,64]{0,2,1:T(8,128)(2,1)} copy(bf16[128,64,64]{2,1,0:T(8,128)(2,1)} %add_convert_fusion) | data formatting | bytes 2097152 | tf_op jit(solution)/shard_map/convert_element_type | solution.py:113
  80.0 3.5 %all-to-all-start = ((bf16[128,4,1024]{0,2,1:T(8,128)(2,1)}), bf16[128,4,1024]{0,2,1:T(8,128)(2,1)S(1)}, u32[]{:S(2)}, u32[]{:S(2)}) async-start(bf16[128,4,1024]{0,2,1:T(8,128)(2,1)} %bitcast.26), calls=%async_computation | async-start | bytes 2097152 | tf_op jit(solution)/shard_map/all_to_all | solution.py:115
  83.9 4.2 %copy.65 = bf16[16,96,576]{1,2,0:T(8,128)(2,1)} copy(bf16[16,96,576]{2,1,0:T(8,128)(2,1)} %param.16) | data formatting | bytes 3538944 | tf_op args[7]
  88.2 0.8 gather_fusion.3
  89.0 19.3 %all-to-all-done = bf16[128,4,1024]{0,2,1:T(8,128)(2,1)S(1)} async-done(((bf16[128,4,1024]{0,2,1:T(8,128)(2,1)}), bf16[128,4,1024]{0,2,1:T(8,128)(2,1)S(1)}, u32[]{:S(2)}, u32[]{:S(2)}) %all-to-all-start) | async-done | bytes 1048608 | tf_op jit(solution)/shard_map/all_to_all | solution.py:115
  108.4 1.3 %copy.61 = bf16[4,128,1024]{2,1,0:T(8,128)(2,1)} copy(bf16[4,128,1024]{1,2,0:T(8,128)(2,1)S(1)} %bitcast.81) | data formatting | bytes 2097152 | tf_op jit(solution)/shard_map/all_to_all | solution.py:115
  109.7 1.5 %convolution_bitcast_fusion.1 = f32[96,1024]{1,0:T(8,128)S(1)} fusion(bf16[512,96]{0,1:T(8,128)(2,1)S(1)} %copy-done, bf16[512,1024]{1,0:T(8,128)(2,1)} %bitcast.82), kind=kOutput, calls=%fused_computation.22 | convolution fusion | flops 100663296 | bytes 1540096 | tf_op jit(solution)/shard_map/ku,kc->uc/dot_general | solution.py:116
  111.4 2.3 %fusion.14 = bf16[96,16,64]{0,2,1:T(8,128)(2,1)S(1)} fusion(f32[96,16,64]{0,2,1:T(8,128)S(1)} %bitcast.85, bf16[96,16,6,64]{0,3,2,1:T(8,128)(2,1)S(1)} %bitcast.78, bf16[16,96,6,96]{1,3,2,0:T(8,128)(2,1)} %bitcast.79, f32[16]{0:T(128)S(1)} %get-tuple-element.31), kind=kOutput, calls=%fused_computation.23 | convolution fusion | flops 113541120 | bytes 3539008 | tf_op jit(solution)/shard_map/sujv,vsjr->usr/dot_general | solution.py:69
  (45 shorter events, 6.5 us)
Async XLA Ops:
  0.0 27.1 %copy-start = (bf16[512,96]{0,1:T(8,128)(2,1)S(1)}, bf16[512,96]{0,1:T(8,128)(2,1)}, u32[]{:S(2)}) copy-start(bf16[512,96]{0,1:T(8,128)(2,1)} %param.11) | copy-start | bytes 294916
  26.4 1.3 %copy-start.7 = (s32[1,2,32]{2,1,0:T(2,128)S(1)}, s32[1,2,32]{2,1,0:T(2,128)}, u32[]{:S(2)}) copy-start(s32[1,2,32]{2,1,0:T(2,128)} %param.13) | copy-start | bytes 772
  30.2 23.5 %collective-permute-start = (bf16[128,2048]{0,1:T(8,128)(2,1)S(1)}, bf16[128,2048]{0,1:T(8,128)(2,1)}, u32[]{:S(2)}, u32[]{:S(2)}) collective-permute-start(bf16[128,2048]{0,1:T(8,128)(2,1)S(1)} %bitcast.86), channel_id=1, source_target_pairs={{0,4},{4,8},{8,12},{12,16},{16,20},{20,24},{24,28},{1,5},{5,9},{9,... | collective-permute-start | bytes 1572872 | tf_op jit(solution)/shard_map/ppermute | solution.py:14
  38.0 6.5 %copy-start.5 = (s32[64,128]{1,0:T(8,128)S(1)}, s32[64,128]{1,0:T(8,128)}, u32[]{:S(2)}) copy-start(s32[64,128]{1,0:T(8,128)} %param.15) | copy-start | bytes 98308
  38.0 20.2 %collective-permute-start.1 = (bf16[128,2048]{0,1:T(8,128)(2,1)}, bf16[128,2048]{0,1:T(8,128)(2,1)}, u32[]{:S(2)}, u32[]{:S(2)}) collective-permute-start(bf16[128,2048]{0,1:T(8,128)(2,1)} %bitcast.24), channel_id=1, source_target_pairs={{4,0},{8,4},{12,8},{16,12},{20,16},{24,20},{28,24},{5,1},{9,5},{13... | collective-permute-start | bytes 1572872 | tf_op jit(solution)/shard_map/ppermute | solution.py:14
  44.5 1.3 %copy-start.8 = (bf16[316,128]{1,0:T(8,128)(2,1)S(1)}, bf16[316,128]{1,0:T(8,128)(2,1)}, u32[]{:S(2)}) copy-start(bf16[316,128]{1,0:T(8,128)(2,1)} %param.12) | copy-start | bytes 242692
  44.5 1.4 %copy-start.9 = (s32[64,128]{1,0:T(8,128)S(1)}, s32[64,128]{1,0:T(8,128)}, u32[]{:S(2)}) copy-start(s32[64,128]{1,0:T(8,128)} %param.14) | copy-start | bytes 98308
  63.5 5.8 %copy-start.1 = (bf16[128,32,64]{1,2,0:T(8,128)(2,1)S(1)}, bf16[128,32,64]{1,2,0:T(8,128)(2,1)}, u32[]{:S(2)}) copy-start(bf16[128,32,64]{1,2,0:T(8,128)(2,1)} %copy.57) | copy-start | bytes 1572868
  63.5 5.8 %copy-start.2 = (bf16[128,64,64]{1,2,0:T(8,128)(2,1)S(1)}, bf16[128,64,64]{1,2,0:T(8,128)(2,1)}, u32[]{:S(2)}) copy-start(bf16[128,64,64]{1,2,0:T(8,128)(2,1)} %copy.55) | copy-start | bytes 3145732
  63.5 5.8 %copy-start.3 = (bf16[64,128,128]{2,1,0:T(8,128)(2,1)S(1)}, bf16[64,128,128]{2,1,0:T(8,128)(2,1)}, u32[]{:S(2)}) copy-start(bf16[64,128,128]{2,1,0:T(8,128)(2,1)} %get-tuple-element.16) | copy-start | bytes 6291460
  75.9 7.6 %copy-start.4 = (bf16[96,1024]{1,0:T(8,128)(2,1)S(1)}, bf16[96,1024]{1,0:T(8,128)(2,1)}, u32[]{:S(2)}) copy-start(bf16[96,1024]{1,0:T(8,128)(2,1)} %param.9) | copy-start | bytes 589828
  75.9 7.8 %copy-start.6 = (s32[16,6]{0,1:T(8,128)S(1)}, s32[16,6]{0,1:T(8,128)}, u32[]{:S(2)}) copy-start(s32[16,6]{0,1:T(8,128)} %param.17) | copy-start | bytes 1156
  80.0 28.4 %all-to-all-start = ((bf16[128,4,1024]{0,2,1:T(8,128)(2,1)}), bf16[128,4,1024]{0,2,1:T(8,128)(2,1)S(1)}, u32[]{:S(2)}, u32[]{:S(2)}) async-start(bf16[128,4,1024]{0,2,1:T(8,128)(2,1)} %bitcast.26), calls=%async_computation | async-start | bytes 2097152 | tf_op jit(solution)/shard_map/all_to_all | solution.py:115
where the time goes:
time: 115 us
  local copies, waits for them, and re-layouts  33.6 us (29%)
  matrix products  24.3 us (21%)
  waiting for transfers between devices  19.3 us (17%)
  blocking collectives  18 us (16%)
  starting transfers between devices  11.9 us (10%)
  other arithmetic  7.11 us (6%)
    all_to_all x1, waiting for transfers between devices, per_device(): lax.all_to_all(incoming, 'dir', split_axis=1, concat_axis=0, tiled=True)  19.3 us
    all_gather x1, blocking collectives, per_device(): gathered = lax.all_gather(masked, 'dir', axis=1, tiled=True)  18 us
    ppermute x2, starting transfers between devices, shifted(): lax.ppermute(value, axis, [(source, source + steps) for source in range(l...  8.37 us
    dot_general x1, matrix products, translate_block(): jnp.einsum('tis,tik->tks', pick_source, values, preferred_element_type=jn...  7.8 us
    dot_general x1, matrix products, translate_block(): jnp.einsum('tks,ksr->ktr', weight_high, extended, preferred_element_type=...  6.58 us
    scatter x2, local copies, waits for them, and re-layouts, per_device(): relayed = jnp.zeros((dir_slice, cluster_slots, rights), jnp.bfloat16).at[...  6.08 us
    dot_general x1, matrix products, translate_block(): jnp.einsum('tks,ksr->ktr', weight_low, extended, preferred_element_type=j...  5.77 us
    reshape x1, local copies, waits for them, and re-layouts, per_device(): from_after.reshape(dir_slice, bound_count, rights)  5.3 us
  transfers between devices with their start and end apart: 3, of which 1 were waited for; matrix products, arithmetic and copies ran while one was open for 22% of the time, Pallas kernels for 0%

commit v1 on v0

v1 whole, which is shorter than its diff:
```python
import jax
import jax.numpy as jnp
from jax import lax
from jax.sharding import PartitionSpec as P


def shifted(value, axis, steps):
    count = lax.axis_size(axis)
    leading, last = (max(0, -steps), min(count, count - steps))
    return lax.ppermute(value, axis, [(source, source + steps) for source in range(leading, last)])


def one_hot(ids, count):
    return (ids[..., None] == jnp.arange(count, dtype=jnp.int32)).astype(jnp.bfloat16)


def per_device(
    sources,
    live_counts,
    aggregate,
    translators,
    boundary_lists,
    far_sources,
    far_translators,
    near_blocks,
    near_columns,
):
    dir_index = lax.axis_index("dir")
    unknowns = sources.shape[0]
    directions = aggregate.shape[0]
    capacity = near_blocks.shape[0]
    rights = sources.shape[1] // capacity
    cluster_slots = far_sources.shape[0]
    neighbours = near_columns.shape[1]
    bound_count = boundary_lists.shape[2]
    f32 = jnp.float32
    counts = live_counts[0]
    own_count = lax.dynamic_index_in_dim(counts, dir_index, 0, keepdims=False)
    own_live = jnp.arange(capacity, dtype=jnp.int32) < own_count
    units = sources.reshape(unknowns, capacity, rights) * own_live.astype(jnp.bfloat16)[None, :, None]
    gathered = lax.all_gather(
        units.reshape(unknowns, capacity * rights), "dir", axis=1, tiled=True
    ).reshape(unknowns, cluster_slots, rights)
    kinds = lax.all_gather(translators, "dir", axis=1, tiled=True)
    passed = jnp.einsum(
        "bms,usr->bumr",
        one_hot(boundary_lists[0], cluster_slots),
        gathered,
        preferred_element_type=f32,
    ).astype(jnp.bfloat16)
    up = shifted(passed[0].reshape(unknowns, -1), "clus", 1)
    down = shifted(passed[1].reshape(unknowns, -1), "clus", -1)
    extended = jnp.concatenate([gathered.reshape(unknowns, -1), up, down], axis=1)
    ext_slots = cluster_slots + 2 * bound_count
    pattern = (
        jnp.dot(aggregate, extended, preferred_element_type=f32)
        .astype(jnp.bfloat16)
        .reshape(directions, ext_slots, rights)
    )
    own_sources = lax.dynamic_slice_in_dim(far_sources, dir_index * capacity, capacity, 0)
    own_kinds = lax.dynamic_slice_in_dim(far_translators, dir_index * capacity, capacity, 0)
    values = jnp.einsum(
        "tin,nk->tik",
        one_hot(own_kinds, kinds.shape[0]),
        kinds,
        preferred_element_type=f32,
    ).astype(jnp.bfloat16)
    weights = jnp.einsum(
        "tis,tik->kts", one_hot(own_sources, ext_slots), values, preferred_element_type=f32
    ).astype(jnp.bfloat16)
    incoming = jnp.einsum("kts,ksr->ktr", weights, pattern, preferred_element_type=f32).astype(
        jnp.bfloat16
    )
    far_part = jnp.dot(
        aggregate.T, incoming.reshape(directions, capacity * rights), preferred_element_type=f32
    )
    stacked = jnp.einsum(
        "sjq,uqr->sjur", one_hot(near_columns, capacity), units, preferred_element_type=f32
    ).astype(jnp.bfloat16)
    near_part = jnp.einsum(
        "suv,svr->usr",
        near_blocks,
        stacked.reshape(capacity, neighbours * unknowns, rights),
        preferred_element_type=f32,
    )
    summed = (far_part.reshape(unknowns, capacity, rights) + near_part) * own_live.astype(f32)[
        None, :, None
    ]
    return summed.reshape(unknowns, capacity * rights).astype(jnp.bfloat16)


def solution(mesh):
    in_specs = (
        P(None, ("clus", "dir")),
        P("clus", None),
        P(),
        P(None, "dir"),
        P("clus", None, None),
        P("clus", None),
        P("clus", None),
        P(("clus", "dir"), None, None),
        P(("clus", "dir"), None),
    )
    out_specs = P(None, ("clus", "dir"))
    return jax.shard_map(
        per_device, mesh=mesh, in_specs=in_specs, out_specs=out_specs, check_vma=False
    )
```

time: 115 us -> 107 us (0.930)
  the two profiles are of different devices: /device:TPU:1 before, /device:TPU:4 now
where the time goes in v1:
time: 107 us; the launch traced here: 106 us
  local copies, waits for them, and re-layouts  34.9 us (33%)
  blocking collectives  34.3 us (32%)
  matrix products  27.7 us (26%)
  starting transfers between devices  6.44 us (6%)
  other arithmetic  2.91 us (3%)
    all_gather x1, blocking collectives, per_device(): lax.all_gather(units.reshape(unknowns, capacity * rights), 'dir', axis=1,...  19.8 us
    all_gather x1, blocking collectives, per_device(): kinds = lax.all_gather(translators, 'dir', axis=1, tiled=True)  14.4 us
    reshape x1, local copies, waits for them, and re-layouts, per_device(): pattern = jnp.dot(aggregate, extended, preferred_element_type=f32).astype...  13.7 us
    dot_general x1, matrix products, per_device(): jnp.einsum('kts,ksr->ktr', weights, pattern, preferred_element_type=f32)  9.83 us
    dot_general x1, matrix products, per_device(): jnp.dot(aggregate, extended, preferred_element_type=f32)  6.71 us
    ppermute x2, starting transfers between devices, shifted(): lax.ppermute(value, axis, [(source, source + steps) for source in range(l...  6.44 us
    reshape x1, local copies, waits for them, and re-layouts, per_device(): stacked.reshape(capacity, neighbours * unknowns, rights)  4.11 us
    dot_general x1, matrix products, per_device(): jnp.einsum('tis,tik->kts', one_hot(own_sources, ext_slots), values, prefe...  3.47 us
  transfers between devices with their start and end apart: 2, of which 0 were waited for; matrix products, arithmetic and copies ran while one was open for 14% of the time, Pallas kernels for 0%

profile of v1, /device:TPU:4, one launch (start us, length us, event | category | flops | bytes accessed | tf_op | source)
XLA Modules:
  0.0 106.3 jit_solution(8265069581036035905)
XLA Ops:
  0.0 1.4 %constant_dynamic-slice_fusion = s32[1,1]{1,0:T(1,128)} fusion(s32[1,4]{1,0:T(1,128)} %param.10, s32[]{:T(128)S(6)} %select_n.9), kind=kLoop, calls=%fused_computation.39 | loop fusion | bytes 12 | tf_op jit(solution)/shard_map/jit(dynamic_index_in_dim)/dynamic_slice | solution.py:38
  1.4 1.2 %compare_convert_fusion = (f32[16]{0:T(128)}, bf16[16]{0:T(256)(128)(2,1)S(1)}) fusion(s32[]{:T(128)} %bitcast.2), kind=kLoop, calls=%fused_computation.37 | loop fusion | flops 48 | bytes 100 | tf_op jit(solution)/shard_map/convert_element_type | solution.py:86
  3.3 0.9 broadcast_multiply_fusion.1
  4.2 19.8 %all_gather.7 = bf16[96,4096]{1,0:T(8,128)(2,1)S(1)} all-gather(bf16[96,1024]{1,0:T(8,128)(2,1)S(1)} %broadcast_multiply_fusion.1), channel_id=1, replica_groups=mesh['clus'=8,'dir'=4] {'dir'}, dimensions={1}, use_global_device_ids=true | all-gather | bytes 983040 | tf_op jit(solution)/shard_map/all_gather | solution.py:41
  24.1 1.3 %copy.26 = bf16[96,4096]{0,1:T(8,128)(2,1)} copy(bf16[96,4096]{1,0:T(8,128)(2,1)S(1)} %all_gather.7) | data formatting | bytes 1572864 | tf_op jit(solution)/shard_map/all_gather | solution.py:41
  25.4 2.1 %fusion.15 = bf16[2,96,32,64]{1,2,0,3:T(8,128)(2,1)S(1)} fusion(bf16[96,64,64,1]{0,2,1,3:T(8,128)(2,1)} %bitcast.53, s32[2,32]{1,0:T(2,128)S(1)} %bitcast.59), kind=kOutput, calls=%fused_computation.16 | convolution fusion | flops 50728960 | bytes 1573120 | tf_op jit(solution)/shard_map/bms,usr->bumr/dot_general | solution.py:45
  27.5 0.9 fusion.34
  28.6 1.0 copy.29
  29.6 1.9 %collective-permute-start = (bf16[96,2048]{1,0:T(8,128)(2,1)}, bf16[96,2048]{1,0:T(8,128)(2,1)}, u32[]{:S(2)}, u32[]{:S(2)}) collective-permute-start(bf16[96,2048]{1,0:T(8,128)(2,1)} %copy.29), channel_id=1, source_target_pairs={{0,4},{4,8},{8,12},{12,16},{16,20},{20,24},{24,28},{1,5},{5,9},{9,... | collective-permute-start | bytes 1179656 | tf_op jit(solution)/shard_map/ppermute | solution.py:10
  31.5 1.2 %copy.30 = bf16[1,96,32,64]{1,3,2,0:T(8,128)(2,1)S(1)} copy(bf16[1,96,32,64]{1,2,0,3:T(8,128)(2,1)} %get-tuple-element.6) | data formatting | bytes 786432 | tf_op jit(solution)/shard_map/slice | solution.py:52
  32.7 1.0 copy.31
  33.7 4.5 %collective-permute-start.1 = (bf16[96,2048]{1,0:T(8,128)(2,1)}, bf16[96,2048]{1,0:T(8,128)(2,1)}, u32[]{:S(2)}, u32[]{:S(2)}) collective-permute-start(bf16[96,2048]{1,0:T(8,128)(2,1)} %copy.31), channel_id=1, source_target_pairs={{4,0},{8,4},{12,8},{16,12},{20,16},{24,20},{28,24},{5,1},{9,5},{13... | collective-permute-start | bytes 1179656 | tf_op jit(solution)/shard_map/ppermute | solution.py:10
  38.4 14.4 %all_gather.6 = bf16[316,512]{1,0:T(8,128)(2,1)} all-gather(bf16[316,128]{1,0:T(8,128)(2,1)S(1)} %copy-done.5), channel_id=1, replica_groups=mesh['clus'=8,'dir'=4] {'dir'}, dimensions={1}, use_global_device_ids=true | all-gather | bytes 404480 | tf_op jit(solution)/shard_map/all_gather | solution.py:44
  53.6 1.3 %convolution_convert_fusion.1 = bf16[16,6,96,64]{2,0,3,1:T(8,128)(2,1)S(1)} fusion(bf16[96,16,64]{0,2,1:T(8,128)(2,1)S(1)} %broadcast_multiply_fusion, s32[16,6]{0,1:T(8,128)} %param.17), kind=kOutput, calls=%fused_computation.9 | convolution fusion | flops 19465728 | bytes 1376640 | tf_op jit(solution)/shard_map/sjq,uqr->sjur/dot_general | solution.py:77
  54.9 2.4 %copy.38 = bf16[16,6,96,64]{2,1,3,0:T(8,128)(2,1)} copy(bf16[16,6,96,64]{2,0,3,1:T(8,128)(2,1)S(1)} %convolution_convert_fusion.1) | data formatting | bytes 2359296 | tf_op jit(solution)/shard_map/convert_element_type | solution.py:79
  57.3 4.1 %reshape.41 = bf16[16,576,64]{1,2,0:T(8,128)(2,1)} reshape(bf16[16,6,96,64]{2,1,3,0:T(8,128)(2,1)} %copy.38) | data formatting | bytes 2359296 | tf_op jit(solution)/shard_map/reshape | solution.py:83
  62.2 3.5 %convert_bitcast_fusion = bf16[512,16,128]{2,0,1:T(8,128)(2,1)} fusion(s32[16,128]{1,0:T(8,128)S(1)} %get-tuple-element.10, s32[16,128]{1,0:T(8,128)S(1)} %get-tuple-element.9, bf16[316,512]{1,0:T(8,128)(2,1)S(1)} %copy-done.4), kind=kOutput, calls=%fused_computation.5 | convolution fusion | flops 934141952 | bytes 2437120 | tf_op jit(solution)/shard_map/tis,tik->kts/dot_general | solution.py:68
  65.7 6.7 %convolution_convert_fusion = bf16[8192,512]{1,0:T(8,128)(2,1)} fusion(bf16[512,96]{0,1:T(8,128)(2,1)S(1)} %copy-done.3, bf16[96,2048]{1,0:T(8,128)(2,1)} %collective-permute-done.1, bf16[96,2048]{1,0:T(8,128)(2,1)} %collective-permute-done, bf16[96,4096]{1,0:T(8,128)(2,1)S(1)} %all_gather.7), kind=kOutput, calls=%fused_computation | convolution fusion | flops 814219264 | bytes 10059776 | tf_op jit(solution)/shard_map/dot_general | solution.py:56
  72.4 13.7 %copy.33 = bf16[512,128,64]{1,2,0:T(8,128)(2,1)} copy(bf16[512,128,64]{0,2,1:T(8,128)(2,1)} %bitcast.51) | data formatting | bytes 16777216 | tf_op jit(solution)/shard_map/reshape | solution.py:58
  86.0 9.8 %fusion.7 = bf16[512,16,64]{2,1,0:T(8,128)(2,1)} fusion(bf16[512,128,64]{1,2,0:T(8,128)(2,1)} %copy.33, bf16[512,16,128]{2,0,1:T(8,128)(2,1)} %convert_bitcast_fusion), kind=kOutput, calls=%fused_computation.8 | convolution fusion | flops 134742016 | bytes 11534336 | tf_op jit(solution)/shard_map/kts,ksr->ktr/dot_general | solution.py:71
  95.8 3.4 %copy.34 = bf16[512,16,64]{0,2,1:T(8,128)(2,1)} copy(bf16[512,16,64]{2,1,0:T(8,128)(2,1)} %fusion.7) | data formatting | bytes 2097152 | tf_op jit(solution)/shard_map/convert_element_type | solution.py:71
  99.3 2.4 %convolution_bitcast_fusion.1 = f32[96,1024]{1,0:T(8,128)} fusion(bf16[512,1024]{0,1:T(8,128)(2,1)} %bitcast.52, bf16[512,96]{0,1:T(8,128)(2,1)S(1)} %copy-done.3), kind=kOutput, calls=%fused_computation.22 | convolution fusion | flops 100663296 | bytes 1540096 | tf_op jit(solution)/shard_map/dot_general | solution.py:74
  101.7 2.0 %copy.35 = f32[96,1024]{0,1:T(8,128)} copy(f32[96,1024]{1,0:T(8,128)} %convolution_bitcast_fusion.1) | data formatting | bytes 786432 | tf_op jit(solution)/shard_map/dot_general | solution.py:74
  103.7 1.8 %fusion.20 = bf16[96,16,64]{0,2,1:T(8,128)(2,1)S(1)} fusion(f32[96,16,64]{0,2,1:T(8,128)} %bitcast.54, bf16[16,576,64]{1,2,0:T(8,128)(2,1)S(1)} %copy-done.1, bf16[16,96,576]{2,1,0:T(8,128)(2,1)S(1)} %copy-done, f32[16]{0:T(128)S(1)} %copy-done.8), kind=kOutput, calls=%fused_computation.21 | convolution fusion | flops 113541120 | bytes 3539008 | tf_op jit(solution)/shard_map/suv,svr->usr/dot_general | solution.py:80
  (27 shorter events, 3.3 us)
Async XLA Ops:
  0.0 103.7 %copy-start = (bf16[16,96,576]{2,1,0:T(8,128)(2,1)S(1)}, bf16[16,96,576]{2,1,0:T(8,128)(2,1)}, u32[]{:S(2)}) copy-start(bf16[16,96,576]{2,1,0:T(8,128)(2,1)} %param.16) | copy-start | bytes 5308420
  0.0 25.4 %copy-start.7 = (s32[1,2,32]{2,1,0:T(2,128)S(1)}, s32[1,2,32]{2,1,0:T(2,128)}, u32[]{:S(2)}) copy-start(s32[1,2,32]{2,1,0:T(2,128)} %param.13) | copy-start | bytes 772
  2.6 0.5 copy-start.6
  28.4 9.8 %copy-start.2 = (bf16[96,1024]{1,0:T(8,128)(2,1)S(1)}, bf16[96,1024]{1,0:T(8,128)(2,1)}, u32[]{:S(2)}) copy-start(bf16[96,1024]{1,0:T(8,128)(2,1)} %param.9) | copy-start | bytes 589828
  28.4 10.0 %copy-start.5 = (bf16[316,128]{1,0:T(8,128)(2,1)S(1)}, bf16[316,128]{1,0:T(8,128)(2,1)}, u32[]{:S(2)}) copy-start(bf16[316,128]{1,0:T(8,128)(2,1)} %param.12) | copy-start | bytes 242692
  29.6 36.1 %collective-permute-start = (bf16[96,2048]{1,0:T(8,128)(2,1)}, bf16[96,2048]{1,0:T(8,128)(2,1)}, u32[]{:S(2)}, u32[]{:S(2)}) collective-permute-start(bf16[96,2048]{1,0:T(8,128)(2,1)} %copy.29), channel_id=1, source_target_pairs={{0,4},{4,8},{8,12},{12,16},{16,20},{20,24},{24,28},{1,5},{5,9},{9,... | collective-permute-start | bytes 1179656 | tf_op jit(solution)/shard_map/ppermute | solution.py:10
  33.7 31.9 %collective-permute-start.1 = (bf16[96,2048]{1,0:T(8,128)(2,1)}, bf16[96,2048]{1,0:T(8,128)(2,1)}, u32[]{:S(2)}, u32[]{:S(2)}) collective-permute-start(bf16[96,2048]{1,0:T(8,128)(2,1)} %copy.31), channel_id=1, source_target_pairs={{4,0},{8,4},{12,8},{16,12},{20,16},{24,20},{28,24},{5,1},{9,5},{13... | collective-permute-start | bytes 1179656 | tf_op jit(solution)/shard_map/ppermute | solution.py:10
  57.3 4.8 %copy-start.4 = (bf16[316,512]{1,0:T(8,128)(2,1)S(1)}, bf16[316,512]{1,0:T(8,128)(2,1)}, u32[]{:S(2)}) copy-start(bf16[316,512]{1,0:T(8,128)(2,1)} %all_gather.6) | copy-start | bytes 970756
  62.2 3.5 %copy-start.3 = (bf16[512,96]{0,1:T(8,128)(2,1)S(1)}, bf16[512,96]{0,1:T(8,128)(2,1)}, u32[]{:S(2)}) copy-start(bf16[512,96]{0,1:T(8,128)(2,1)} %param.11) | copy-start | bytes 294916
  95.8 7.8 %copy-start.1 = (bf16[16,576,64]{1,2,0:T(8,128)(2,1)S(1)}, bf16[16,576,64]{1,2,0:T(8,128)(2,1)}, u32[]{:S(2)}) copy-start(bf16[16,576,64]{1,2,0:T(8,128)(2,1)} %reshape.41) | copy-start | bytes 3538948
  95.8 7.8 %copy-start.8 = (f32[16]{0:T(128)S(1)}, f32[16]{0:T(128)}, u32[]{:S(2)}) copy-start(f32[16]{0:T(128)} %get-tuple-element.7) | copy-start | bytes 196

commit v2 on v1

v2 whole, which is shorter than its diff:
```python
import functools

import jax
import jax.numpy as jnp
from jax import lax
from jax.experimental import pallas as pl
from jax.experimental.pallas import tpu as pltpu
from jax.sharding import PartitionSpec as P

LANES = 128
F32 = jnp.float32
BF16 = jnp.bfloat16
VMEM = pltpu.VMEM
SMEM = pltpu.SMEM


def exchange(n_dir, n_clus, pair_ref, half_ref, units_ref, table_ref, all_ref, before_ref, after_ref,
             kinds_ref, up_ref, down_ref, send_sem, recv_sem, tsend_sem, trecv_sem, bsend_sem, brecv_sem):
    me = lax.axis_index("dir")
    cluster = lax.axis_index("clus")
    has_before = cluster > 0
    has_after = cluster < n_clus - 1
    pairs = units_ref.shape[0]
    rows = table_ref.shape[0]
    barrier = pltpu.get_barrier_semaphore()
    for step in range(1, n_dir):
        pl.semaphore_signal(barrier, inc=1, device_id={"dir": lax.rem(me + step, n_dir)},
                            device_id_type=pl.DeviceIdType.MESH)

    @pl.when(has_before)
    def _():
        pl.semaphore_signal(barrier, inc=1, device_id={"clus": cluster - 1},
                            device_id_type=pl.DeviceIdType.MESH)

    @pl.when(has_after)
    def _():
        pl.semaphore_signal(barrier, inc=1, device_id={"clus": cluster + 1},
                            device_id_type=pl.DeviceIdType.MESH)

    sides = has_before.astype(jnp.int32) + has_after.astype(jnp.int32)
    pl.semaphore_wait(barrier, n_dir - 1 + sides)

    own = pl.ds(me * pairs, pairs)
    own_rows = pl.ds(pl.multiple_of(me * rows, rows), rows)
    copies = []
    for src, dst, ss, rs in (
        (units_ref, all_ref.at[own], send_sem, recv_sem),
        (table_ref, kinds_ref.at[own_rows], tsend_sem, trecv_sem),
    ):
        for step in range(1, n_dir):
            copy = pltpu.make_async_remote_copy(
                src_ref=src, dst_ref=dst, send_sem=ss.at[step], recv_sem=rs.at[step],
                device_id={"dir": lax.rem(me + step, n_dir)}, device_id_type=pl.DeviceIdType.MESH)
            copy.start()
            copies.append(copy)
    all_ref[own] = units_ref[...]
    kinds_ref[own_rows] = table_ref[...]

    @pl.when(jnp.logical_not(has_before))
    def _():
        before_ref[...] = jnp.zeros_like(before_ref)

    @pl.when(jnp.logical_not(has_after))
    def _():
        after_ref[...] = jnp.zeros_like(after_ref)

    for copy in copies[: n_dir - 1]:
        copy.wait_recv()
    width = units_ref.shape[2] // 2

    def pick(row, m):
        value = all_ref[pair_ref[row, m]]
        return jnp.where(half_ref[row, m] == 1, value[:, width:], value[:, :width])

    upward = pltpu.make_async_remote_copy(
        src_ref=up_ref, dst_ref=before_ref, send_sem=bsend_sem.at[0], recv_sem=brecv_sem.at[0],
        device_id={"clus": cluster + 1}, device_id_type=pl.DeviceIdType.MESH)
    downward = pltpu.make_async_remote_copy(
        src_ref=down_ref, dst_ref=after_ref, send_sem=bsend_sem.at[1], recv_sem=brecv_sem.at[1],
        device_id={"clus": cluster - 1}, device_id_type=pl.DeviceIdType.MESH)
    for row, (ref, there, copy) in enumerate(
        ((up_ref, has_after, upward), (down_ref, has_before, downward))
    ):
        def fill(p, carry, row=row, ref=ref):
            ref[p] = jnp.concatenate([pick(row, 2 * p), pick(row, 2 * p + 1)], axis=1)
            return carry

        lax.fori_loop(0, ref.shape[0], fill, 0)

        @pl.when(there)
        def _(copy=copy):
            copy.start()

    for copy in copies[n_dir - 1 :]:
        copy.wait_recv()
    for copy in copies:
        copy.wait_send()

    @pl.when(has_after)
    def _():
        upward.wait_send()
        downward.wait_recv()

    @pl.when(has_before)
    def _():
        downward.wait_send()
        upward.wait_recv()


def compute(count_ref, near_cols_ref, all_ref, before_ref, after_ref, kinds_ref, agg_ref, aggt_ref,
            units_ref, src_ids_ref, kind_ids_ref, near_ref, out_ref, e_ref, w_ref, inc_ref, acc_ref, near_acc_ref,
            local_ref, stack_ref):
    step = pl.program_id(0)
    block = agg_ref.shape[0]
    capacity, unknowns, rights = local_ref.shape
    own_pairs, bound_pairs = all_ref.shape[0], before_ref.shape[0]
    pairs = own_pairs + 2 * bound_pairs
    chunk = near_ref.shape[0]
    neighbours = near_cols_ref.shape[1]
    interactions = src_ids_ref.shape[1]

    @pl.when(step == 0)
    def _():
        acc_ref[...] = jnp.zeros_like(acc_ref)
        for s in range(capacity):
            lo = (s % 2) * rights
            local_ref[s] = units_ref[s // 2, :, lo : lo + rights]

    rows = agg_ref[...]

    def patterns(ref, first):
        def body(p, carry):
            two = jnp.concatenate([ref[2 * p], ref[2 * p + 1]], axis=1)
            made = jnp.dot(rows, two, preferred_element_type=F32)
            at = pl.multiple_of((first + 2 * p) * block, block)
            e_ref[pl.ds(at, block), :] = made[:, :LANES]
            e_ref[pl.ds(at + block, block), :] = made[:, LANES:]
            return carry

        lax.fori_loop(0, ref.shape[0] // 2, body, 0, unroll=4)

    patterns(all_ref, 0)
    patterns(before_ref, own_pairs)
    patterns(after_ref, own_pairs + bound_pairs)

    table = kinds_ref[...]
    kind_rows = lax.broadcasted_iota(jnp.int32, (table.shape[1], interactions), 0)
    place = lax.broadcasted_iota(jnp.int32, (2 * pairs, interactions), 0)
    slot_rows = jnp.where(place < pairs, 2 * place, 2 * (place - pairs) + 1)

    def weigh(t, carry):
        pick_kind = jnp.where(kind_rows == kind_ids_ref[pl.ds(t, 1), :], 1.0, 0.0).astype(BF16)
        values = jnp.dot(table, pick_kind, preferred_element_type=F32).astype(BF16)
        pick_source = jnp.where(slot_rows == src_ids_ref[pl.ds(t, 1), :], 1.0, 0.0).astype(BF16)
        made = lax.dot_general(values, pick_source, (((1,), (1,)), ((), ())),
                               preferred_element_type=F32)
        for half in range(2):
            at = pl.multiple_of((half * capacity + t) * block, block)
            for c in range(w_ref.shape[0]):
                lo, hi = c * LANES, min((c + 1) * LANES, pairs)
                w_ref[c, pl.ds(at, block), : hi - lo] = made[:, half * pairs + lo : half * pairs + hi]
        return carry

    lax.fori_loop(0, capacity, weigh, 0, unroll=2)

    def translate(k, carry):
        e = e_ref[pl.ds(k, pairs, stride=block), :].astype(BF16)
        w = [w_ref[c, pl.ds(k, 2 * capacity, stride=block), :] for c in range(w_ref.shape[0])]
        w = jnp.concatenate(w, axis=1)[:, :pairs].astype(BF16)
        o = jnp.dot(w, e, preferred_element_type=F32)
        at = pl.multiple_of(k * capacity, capacity)
        inc_ref[pl.ds(at, capacity), :rights] = o[:capacity, :rights] + o[capacity:, rights:]
        return carry

    lax.fori_loop(0, block, translate, 0, unroll=8)

    columns = aggt_ref[...]
    for p in range(capacity // 2):
        two = [inc_ref[pl.ds(2 * p + h, block, stride=capacity), :][:, :rights] for h in range(2)]
        two = jnp.concatenate(two, axis=1).astype(BF16)
        acc_ref[p] += jnp.dot(columns, two, preferred_element_type=F32)

    for p in range(chunk // 2):
        parts = []
        for h in range(2):
            s = step * chunk + 2 * p + h
            for j in range(neighbours):
                stack_ref[h, j * unknowns : (j + 1) * unknowns, :] = local_ref[near_cols_ref[s, j]]
            parts.append(jnp.dot(near_ref[2 * p + h], stack_ref[h], preferred_element_type=F32))
        near_acc_ref[step * (chunk // 2) + p] = jnp.concatenate(parts, axis=1)

    @pl.when(step == pl.num_programs(0) - 1)
    def _():
        side = lax.broadcasted_iota(jnp.int32, (unknowns, LANES), 1) // rights
        for p in range(capacity // 2):
            total = jnp.where(side + 2 * p < count_ref[0], acc_ref[p] + near_acc_ref[p], 0.0)
            out_ref[:, p * LANES : (p + 1) * LANES] = total.astype(BF16)


def per_device(
    sources,
    live_counts,
    aggregate,
    translators,
    boundary_lists,
    far_sources,
    far_translators,
    near_blocks,
    near_columns,
):
    n_dir, n_clus = lax.axis_size("dir"), lax.axis_size("clus")
    dir_index = lax.axis_index("dir")
    unknowns = sources.shape[0]
    directions = aggregate.shape[0]
    capacity = near_blocks.shape[0]
    rights = sources.shape[1] // capacity
    slots, interactions = far_sources.shape
    neighbours = near_columns.shape[1]
    bound = boundary_lists.shape[2]
    dir_slice = translators.shape[1]
    block = LANES
    steps = directions // block
    chunk = capacity // steps
    pairs = (slots + 2 * bound) // 2
    own_count = lax.dynamic_slice_in_dim(live_counts[0], dir_index, 1, 0)
    live = jnp.arange(capacity, dtype=jnp.int32) < own_count[0]
    units = sources.reshape(unknowns, capacity, rights) * live.astype(BF16)[None, :, None]
    units = units.reshape(unknowns, capacity // 2, 2 * rights).transpose(1, 0, 2)
    kind_width = -(-translators.shape[0] // LANES) * LANES
    table = jnp.pad(translators.T, ((0, 0), (0, kind_width - translators.shape[0])))
    sent = (bound // 2, unknowns, 2 * rights)
    gathered, before, after, kinds = pl.pallas_call(
        functools.partial(exchange, n_dir, n_clus),
        out_shape=[
            jax.ShapeDtypeStruct((slots // 2, unknowns, 2 * rights), BF16),
            jax.ShapeDtypeStruct(sent, BF16),
            jax.ShapeDtypeStruct(sent, BF16),
            jax.ShapeDtypeStruct((directions, kind_width), BF16),
        ],
        in_specs=[pl.BlockSpec(memory_space=SMEM)] * 2 + [pl.BlockSpec(memory_space=VMEM)] * 2,
        out_specs=[pl.BlockSpec(memory_space=VMEM)] * 4,
        scratch_shapes=[VMEM(sent, BF16), VMEM(sent, BF16)]
        + [pltpu.SemaphoreType.DMA((n_dir,))] * 4
        + [pltpu.SemaphoreType.DMA((2,))] * 2,
        compiler_params=pltpu.CompilerParams(
            collective_id=0, has_side_effects=True, vmem_limit_bytes=32 * 2**20
        ),
        name="exchange",
    )(boundary_lists[0] // 2, boundary_lists[0] % 2, units, table)
    own_sources = lax.dynamic_slice_in_dim(far_sources, dir_index * capacity, capacity, 0)
    own_kinds = lax.dynamic_slice_in_dim(far_translators, dir_index * capacity, capacity, 0)

    def whole(shape):
        return pl.BlockSpec(shape, lambda i: (0,) * len(shape))

    return pl.pallas_call(
        compute,
        grid=(steps,),
        out_shape=jax.ShapeDtypeStruct((unknowns, capacity * rights), BF16),
        in_specs=[
            pl.BlockSpec(memory_space=SMEM),
            pl.BlockSpec(memory_space=SMEM),
            whole(gathered.shape),
            whole(before.shape),
            whole(after.shape),
            pl.BlockSpec((block, kind_width), lambda i: (i, 0)),
            pl.BlockSpec((block, unknowns), lambda i: (i, 0)),
            pl.BlockSpec((unknowns, block), lambda i: (0, i)),
            whole(units.shape),
            whole(own_sources.shape),
            whole(own_kinds.shape),
            pl.BlockSpec((chunk, unknowns, neighbours * unknowns), lambda i: (i, 0, 0)),
        ],
        out_specs=whole((unknowns, capacity * rights)),
        scratch_shapes=[
            VMEM((pairs * block, LANES), F32),
            VMEM((-(-pairs // LANES), 2 * capacity * block, LANES), F32),
            VMEM((block * capacity, LANES), F32),
            VMEM((capacity // 2, unknowns, LANES), F32),
            VMEM((capacity // 2, unknowns, LANES), F32),
            VMEM((capacity, unknowns, rights), BF16),
            VMEM((2, neighbours * unknowns, rights), BF16),
        ],
        compiler_params=pltpu.CompilerParams(vmem_limit_bytes=48 * 2**20),
        name="compute",
    )(own_count, near_columns, gathered, before, after, kinds, aggregate, aggregate.T, units,
      own_sources, own_kinds, near_blocks)


def solution(mesh):
    in_specs = (
        P(None, ("clus", "dir")),
        P("clus", None),
        P(),
        P(None, "dir"),
        P("clus", None, None),
        P("clus", None),
        P("clus", None),
        P(("clus", "dir"), None, None),
        P(("clus", "dir"), None),
    )
    out_specs = P(None, ("clus", "dir"))
    return jax.shard_map(
        per_device, mesh=mesh, in_specs=in_specs, out_specs=out_specs, check_vma=False
    )
```

time: 107 us -> 101 us (0.944)
  the two profiles are of different devices: /device:TPU:4 before, /device:TPU:9 now
where the time goes in v2:
time: 101 us; the launch traced here: 100 us
  Pallas kernels  91.7 us (91%)
  local copies, waits for them, and re-layouts  7.37 us (7%)
  other arithmetic  1.3 us (1%)
    pallas_call x1, Pallas kernels, per_device(): pl.pallas_call(compute, grid=(steps,), out_shape=jax.ShapeDtypeStruct((un...  53 us
    pallas_call x1, Pallas kernels, per_device(): pl.pallas_call(functools.partial(exchange, n_dir, n_clus), out_shape=[jax...  38.7 us
    unnamed x9, local copies, waits for them, and re-layouts  5.21 us

profile of v2, /device:TPU:9, one launch (start us, length us, event | category | flops | bytes accessed | tf_op | source)
XLA Modules:
  0.0 100.5 jit_solution(1054208030396868991)
XLA Ops:
  0.0 0.0 copy-start
  0.0 1.3 %constant_dynamic-slice_fusion.2 = s32[1,1]{1,0:T(1,128)} fusion(s32[1,4]{1,0:T(1,128)} %param.10, s32[]{:T(128)S(6)} %select_n.19), kind=kLoop, calls=%fused_computation.13 | loop fusion | bytes 12 | tf_op jit(solution)/shard_map/dynamic_slice | solution.py:225
  1.3 0.6 fusion.1
  1.8 0.1 mul.17
  1.9 0.1 mul.18
  2.0 0.7 and_select_fusion
  2.7 0.8 copy.15.near_cols_ref
  3.5 0.7 constant_dynamic-slice_fusion
  4.2 1.0 copy.14
  5.2 1.0 %copy.16.agg_ref = bf16[512,96]{1,0:T(8,128)(2,1)S(1)} copy(bf16[512,96]{0,1:T(8,128)(2,1)} %param.11) | data formatting | bytes 196608 | tf_op args[2]
  6.2 0.0 copy-done
  6.3 38.7 %exchange.1 = (bf16[32,96,128]{2,1,0:T(8,128)(2,1)S(1)}, bf16[16,96,128]{2,1,0:T(8,128)(2,1)S(1)}, bf16[16,96,128]{2,1,0:T(8,128)(2,1)S(1)}, bf16[512,384]{1,0:T(8,128)(2,1)S(1)}) custom-call(s32[2,32]{1,0:T(2,128)S(1)} %get-tuple-element.14.pair_ref, s32[2,32]{1,0:T(2,128)S(1)} %get-tuple-element.13.half_ref, bf16[8,96,128]{2,1,0:T(8,128)(2,1)S(1)} %fusion.units_ref, ...), custom_call_target="tpu_custom_call" | custom-call | tf_op jit(solution)/shard_map/exchange/pallas_call | solution.py:232
  45.0 0.0 copy-start.1
  45.0 1.5 %copy-done.1 = bf16[16,96,576]{2,1,0:T(8,128)(2,1)S(1)} copy-done((bf16[16,96,576]{2,1,0:T(8,128)(2,1)S(1)}, bf16[16,96,576]{2,1,0:T(8,128)(2,1)}, u32[]{:S(2)}) %copy-start.1) | copy-done | bytes 1769496
  46.5 0.0 copy-start.2
  46.5 0.9 copy-done.2
  47.4 53.0 %compute.1 = bf16[96,1024]{1,0:T(8,128)(2,1)} custom-call(s32[1]{0:T(128)} %bitcast.count_ref, s32[16,6]{1,0:T(8,128)S(1)} %copy.15.near_cols_ref, bf16[32,96,128]{2,1,0:T(8,128)(2,1)S(1)} %get-tuple-element.9.all_ref, bf16[16,96,128]{2,1,0:T(8,128)(2,1)S(1)} %get-tuple-element.10.before_ref, bf16[16,96,128]{2,1,0:T(8,128)(2,1)S(1)} %get-tuple-element.11.after_ref, ...), custom_call_target="tpu_custom_call" | custom-call | tf_op jit(solution)/shard_map/compute/pallas_call | solution.py:256
  (2 shorter events, 0.1 us)
Async XLA Ops:
  0.0 6.2 %copy-start = (bf16[96,1024]{1,0:T(8,128)(2,1)S(1)}, bf16[96,1024]{1,0:T(8,128)(2,1)}, u32[]{:S(2)}) copy-start(bf16[96,1024]{1,0:T(8,128)(2,1)} %param.9) | copy-start | bytes 589828
  45.0 1.5 %copy-start.1 = (bf16[16,96,576]{2,1,0:T(8,128)(2,1)S(1)}, bf16[16,96,576]{2,1,0:T(8,128)(2,1)}, u32[]{:S(2)}) copy-start(bf16[16,96,576]{2,1,0:T(8,128)(2,1)} %near_ref.1) | copy-start | bytes 5308420
  46.5 0.9 copy-start.2

commit v3 on v2

--- a/solution.py
+++ b/solution.py
@@ -8,6 +8,8 @@
 from jax.sharding import PartitionSpec as P
 
 LANES = 128
+GAP = 8
+SCRATCH_BYTES = 32 * 2**20
 F32 = jnp.float32
 BF16 = jnp.bfloat16
 VMEM = pltpu.VMEM
@@ -112,6 +114,7 @@
             local_ref, stack_ref):
     step = pl.program_id(0)
     block = agg_ref.shape[0]
+    stride = block + GAP
     capacity, unknowns, rights = local_ref.shape
     own_pairs, bound_pairs = all_ref.shape[0], before_ref.shape[0]
     pairs = own_pairs + 2 * bound_pairs
@@ -132,12 +135,12 @@
         def body(p, carry):
             two = jnp.concatenate([ref[2 * p], ref[2 * p + 1]], axis=1)
             made = jnp.dot(rows, two, preferred_element_type=F32)
-            at = pl.multiple_of((first + 2 * p) * block, block)
+            at = pl.multiple_of((first + 2 * p) * stride, GAP)
             e_ref[pl.ds(at, block), :] = made[:, :LANES]
-            e_ref[pl.ds(at + block, block), :] = made[:, LANES:]
+            e_ref[pl.ds(at + stride, block), :] = made[:, LANES:]
             return carry
 
-        lax.fori_loop(0, ref.shape[0] // 2, body, 0, unroll=4)
+        lax.fori_loop(0, ref.shape[0] // 2, body, 0, unroll=8)
 
     patterns(all_ref, 0)
     patterns(before_ref, own_pairs)
@@ -155,24 +158,24 @@
         made = lax.dot_general(values, pick_source, (((1,), (1,)), ((), ())),
                                preferred_element_type=F32)
         for half in range(2):
-            at = pl.multiple_of((half * capacity + t) * block, block)
+            at = pl.multiple_of((half * capacity + t) * stride, GAP)
             for c in range(w_ref.shape[0]):
                 lo, hi = c * LANES, min((c + 1) * LANES, pairs)
                 w_ref[c, pl.ds(at, block), : hi - lo] = made[:, half * pairs + lo : half * pairs + hi]
         return carry
 
-    lax.fori_loop(0, capacity, weigh, 0, unroll=2)
+    lax.fori_loop(0, capacity, weigh, 0, unroll=8)
 
     def translate(k, carry):
-        e = e_ref[pl.ds(k, pairs, stride=block), :].astype(BF16)
-        w = [w_ref[c, pl.ds(k, 2 * capacity, stride=block), :] for c in range(w_ref.shape[0])]
+        e = e_ref[pl.ds(k, pairs, stride=stride), :].astype(BF16)
+        w = [w_ref[c, pl.ds(k, 2 * capacity, stride=stride), :] for c in range(w_ref.shape[0])]
         w = jnp.concatenate(w, axis=1)[:, :pairs].astype(BF16)
         o = jnp.dot(w, e, preferred_element_type=F32)
         at = pl.multiple_of(k * capacity, capacity)
         inc_ref[pl.ds(at, capacity), :rights] = o[:capacity, :rights] + o[capacity:, rights:]
         return carry
 
-    lax.fori_loop(0, block, translate, 0, unroll=8)
+    lax.fori_loop(0, block, translate, 0, unroll=64)
 
     columns = aggt_ref[...]
     for p in range(capacity // 2):
@@ -218,10 +221,14 @@
     neighbours = near_columns.shape[1]
     bound = boundary_lists.shape[2]
     dir_slice = translators.shape[1]
-    block = LANES
+    pairs = (slots + 2 * bound) // 2
+    weight_groups = -(-pairs // LANES)
+    row_bytes = (pairs + weight_groups * 2 * capacity) * LANES * 4
+    block = directions
+    while block > LANES and row_bytes * block > SCRATCH_BYTES:
+        block //= 2
     steps = directions // block
     chunk = capacity // steps
-    pairs = (slots + 2 * bound) // 2
     own_count = lax.dynamic_slice_in_dim(live_counts[0], dir_index, 1, 0)
     live = jnp.arange(capacity, dtype=jnp.int32) < own_count[0]
     units = sources.reshape(unknowns, capacity, rights) * live.astype(BF16)[None, :, None]
@@ -273,15 +280,15 @@
         ],
         out_specs=whole((unknowns, capacity * rights)),
         scratch_shapes=[
-            VMEM((pairs * block, LANES), F32),
-            VMEM((-(-pairs // LANES), 2 * capacity * block, LANES), F32),
+            VMEM((pairs * (block + GAP), LANES), F32),
+            VMEM((weight_groups, 2 * capacity * (block + GAP), LANES), F32),
             VMEM((block * capacity, LANES), F32),
             VMEM((capacity // 2, unknowns, LANES), F32),
             VMEM((capacity // 2, unknowns, LANES), F32),
             VMEM((capacity, unknowns, rights), BF16),
             VMEM((2, neighbours * unknowns, rights), BF16),
         ],
-        compiler_params=pltpu.CompilerParams(vmem_limit_bytes=48 * 2**20),
+        compiler_params=pltpu.CompilerParams(vmem_limit_bytes=56 * 2**20),
         name="compute",
     )(own_count, near_columns, gathered, before, after, kinds, aggregate, aggregate.T, units,
       own_sources, own_kinds, near_blocks)

time: 101 us -> 67.9 us (0.67)
  Pallas kernels: 91.7 us -> 56.2 us
  local copies, waits for them, and re-layouts: 7.37 us -> 9.98 us
    pallas_call x1, Pallas kernels: 53 us -> 17.5 us  [per_device(): pl.pallas_call(compute, grid=(steps,), out_shape=jax.ShapeDtypeStruct((un...]
    unnamed x9 -> x15, local copies, waits for them, and re-layouts: 5.21 us -> 7.16 us
where the time goes in v3:
time: 67.9 us; the launch traced here: 67.6 us
  Pallas kernels  56.2 us (83%)
  local copies, waits for them, and re-layouts  9.98 us (15%)
  other arithmetic  1.37 us (2%)
    pallas_call x1, Pallas kernels, per_device(): pl.pallas_call(functools.partial(exchange, n_dir, n_clus), out_shape=[jax...  38.7 us
    pallas_call x1, Pallas kernels, per_device(): pl.pallas_call(compute, grid=(steps,), out_shape=jax.ShapeDtypeStruct((un...  17.5 us
    unnamed x15, local copies, waits for them, and re-layouts  7.16 us

profile of v3, /device:TPU:9, one launch (start us, length us, event | category | flops | bytes accessed | tf_op | source)
XLA Modules:
  0.0 67.6 jit_solution(6421945182956343611)
XLA Ops:
  0.0 0.0 copy-start
  0.0 1.3 %constant_dynamic-slice_fusion.2 = s32[1,1]{1,0:T(1,128)} fusion(s32[1,4]{1,0:T(1,128)} %param.10, s32[]{:T(128)S(6)} %select_n.19), kind=kLoop, calls=%fused_computation.13 | loop fusion | bytes 12 | tf_op jit(solution)/shard_map/dynamic_slice | solution.py:232
  1.3 0.6 fusion.1
  2.0 0.1 mul.17
  2.0 0.1 mul.18
  2.1 0.7 %and_select_fusion = (s32[2,32]{1,0:T(2,128)S(1)}, s32[2,32]{1,0:T(2,128)S(1)}) fusion(s32[1,2,32]{2,1,0:T(2,128)} %param.13), kind=kLoop, calls=%fused_computation.4 | loop fusion | flops 1216 | bytes 768 | tf_op jit(solution)/shard_map/jit(remainder)/select_n | solution.py:256
  2.8 1.4 %copy.15.near_cols_ref = s32[16,6]{1,0:T(8,128)} copy(s32[16,6]{0,1:T(8,128)} %param.17) | data formatting | bytes 768 | tf_op args[8]
  4.2 1.3 %constant_dynamic-slice_fusion = (s32[16,128]{1,0:T(8,128)}, s32[16,128]{1,0:T(8,128)}) fusion(s32[64,128]{1,0:T(8,128)} %param.15, s32[]{:T(128)S(6)} %select_n.22, s32[64,128]{1,0:T(8,128)} %param.14), kind=kLoop, calls=%fused_computation.11 | loop fusion | bytes 32772 | tf_op jit(solution)/shard_map/dynamic_slice | solution.py:258
  5.5 1.0 %copy.14 = bf16[316,128]{0,1:T(8,128)(2,1)S(1)} copy(bf16[316,128]{1,0:T(8,128)(2,1)} %param.12) | data formatting | bytes 161792 | tf_op args[3]
  6.5 1.6 %copy.16.agg_ref = bf16[512,96]{1,0:T(8,128)(2,1)} copy(bf16[512,96]{0,1:T(8,128)(2,1)} %param.11) | data formatting | bytes 196608 | tf_op args[2]
  8.2 0.0 copy-done
  8.2 0.0 copy-start.1
  8.2 38.7 %exchange.1 = (bf16[32,96,128]{2,1,0:T(8,128)(2,1)S(1)}, bf16[16,96,128]{2,1,0:T(8,128)(2,1)S(1)}, bf16[16,96,128]{2,1,0:T(8,128)(2,1)S(1)}, bf16[512,384]{1,0:T(8,128)(2,1)S(1)}) custom-call(s32[2,32]{1,0:T(2,128)S(1)} %get-tuple-element.14.pair_ref, s32[2,32]{1,0:T(2,128)S(1)} %get-tuple-element.13.half_ref, bf16[8,96,128]{2,1,0:T(8,128)(2,1)S(1)} %fusion.units_ref, ...), custom_call_target="tpu_custom_call" | custom-call | tf_op jit(solution)/shard_map/exchange/pallas_call | solution.py:239
  46.9 0.0 copy-start.2
  46.9 0.9 %copy-done.2 = bf16[32,96,128]{2,1,0:T(8,128)(2,1)} copy-done((bf16[32,96,128]{2,1,0:T(8,128)(2,1)}, bf16[32,96,128]{2,1,0:T(8,128)(2,1)S(1)}, u32[]{:S(2)}) %copy-start.2) | copy-done | bytes 786456
  47.8 0.0 copy-start.3
  47.8 0.8 %copy-done.3 = bf16[16,96,128]{2,1,0:T(8,128)(2,1)} copy-done((bf16[16,96,128]{2,1,0:T(8,128)(2,1)}, bf16[16,96,128]{2,1,0:T(8,128)(2,1)S(1)}, u32[]{:S(2)}) %copy-start.3) | copy-done | bytes 393240
  48.6 0.0 copy-start.4
  48.6 0.8 %copy-done.4 = bf16[16,96,128]{2,1,0:T(8,128)(2,1)} copy-done((bf16[16,96,128]{2,1,0:T(8,128)(2,1)}, bf16[16,96,128]{2,1,0:T(8,128)(2,1)S(1)}, u32[]{:S(2)}) %copy-start.4) | copy-done | bytes 393240
  49.3 0.0 copy-start.5
  49.3 0.7 %copy-done.5 = bf16[512,384]{1,0:T(8,128)(2,1)} copy-done((bf16[512,384]{1,0:T(8,128)(2,1)}, bf16[512,384]{1,0:T(8,128)(2,1)S(1)}, u32[]{:S(2)}) %copy-start.5) | copy-done | bytes 393240
  50.1 0.0 copy-done.1
  50.1 17.5 %compute.1 = bf16[96,1024]{1,0:T(8,128)(2,1)} custom-call(s32[1]{0:T(128)} %bitcast.count_ref, s32[16,6]{1,0:T(8,128)} %copy.15.near_cols_ref, bf16[32,96,128]{2,1,0:T(8,128)(2,1)} %copy-done.2, bf16[16,96,128]{2,1,0:T(8,128)(2,1)} %copy-done.3, bf16[16,96,128]{2,1,0:T(8,128)(2,1)} %copy-done.4, bf16[512,384]{1,0:T(8,128)(2,1)} %copy-done.5, ...), custom_call_target="tpu_custom_call" | custom-call | tf_op jit(solution)/shard_map/compute/pallas_call | solution.py:263
  (2 shorter events, 0.1 us)
Async XLA Ops:
  0.0 8.2 %copy-start = (bf16[96,1024]{1,0:T(8,128)(2,1)S(1)}, bf16[96,1024]{1,0:T(8,128)(2,1)}, u32[]{:S(2)}) copy-start(bf16[96,1024]{1,0:T(8,128)(2,1)} %param.9) | copy-start | bytes 589828
  8.2 41.9 %copy-start.1 = (bf16[8,96,128]{2,1,0:T(8,128)(2,1)}, bf16[8,96,128]{2,1,0:T(8,128)(2,1)S(1)}, u32[]{:S(2)}) copy-start(bf16[8,96,128]{2,1,0:T(8,128)(2,1)S(1)} %fusion.units_ref) | copy-start | bytes 589828
  46.9 0.9 %copy-start.2 = (bf16[32,96,128]{2,1,0:T(8,128)(2,1)}, bf16[32,96,128]{2,1,0:T(8,128)(2,1)S(1)}, u32[]{:S(2)}) copy-start(bf16[32,96,128]{2,1,0:T(8,128)(2,1)S(1)} %get-tuple-element.9.all_ref) | copy-start | bytes 2359300
  47.8 0.8 %copy-start.3 = (bf16[16,96,128]{2,1,0:T(8,128)(2,1)}, bf16[16,96,128]{2,1,0:T(8,128)(2,1)S(1)}, u32[]{:S(2)}) copy-start(bf16[16,96,128]{2,1,0:T(8,128)(2,1)S(1)} %get-tuple-element.10.before_ref) | copy-start | bytes 1179652
  48.6 0.8 %copy-start.4 = (bf16[16,96,128]{2,1,0:T(8,128)(2,1)}, bf16[16,96,128]{2,1,0:T(8,128)(2,1)S(1)}, u32[]{:S(2)}) copy-start(bf16[16,96,128]{2,1,0:T(8,128)(2,1)S(1)} %get-tuple-element.11.after_ref) | copy-start | bytes 1179652
  49.3 0.8 %copy-start.5 = (bf16[512,384]{1,0:T(8,128)(2,1)}, bf16[512,384]{1,0:T(8,128)(2,1)S(1)}, u32[]{:S(2)}) copy-start(bf16[512,384]{1,0:T(8,128)(2,1)S(1)} %get-tuple-element.12.kinds_ref) | copy-start | bytes 1179652

commit v4 on v3

--- a/solution.py
+++ b/solution.py
@@ -8,6 +8,7 @@
 from jax.sharding import PartitionSpec as P
 
 LANES = 128
+CHUNKS = 2
 GAP = 8
 SCRATCH_BYTES = 32 * 2**20
 F32 = jnp.float32
@@ -44,20 +45,36 @@
 
     own = pl.ds(me * pairs, pairs)
     own_rows = pl.ds(pl.multiple_of(me * rows, rows), rows)
-    copies = []
-    for src, dst, ss, rs in (
-        (units_ref, all_ref.at[own], send_sem, recv_sem),
-        (table_ref, kinds_ref.at[own_rows], tsend_sem, trecv_sem),
-    ):
-        for step in range(1, n_dir):
-            copy = pltpu.make_async_remote_copy(
-                src_ref=src, dst_ref=dst, send_sem=ss.at[step], recv_sem=rs.at[step],
-                device_id={"dir": lax.rem(me + step, n_dir)}, device_id_type=pl.DeviceIdType.MESH)
-            copy.start()
-            copies.append(copy)
     all_ref[own] = units_ref[...]
     kinds_ref[own_rows] = table_ref[...]
-
+    part = pairs // CHUNKS
+
+    def hop(side, distance, chunk):
+        sign = 1 - 2 * side
+        owner = me - sign * (distance - 1)
+        target = me + sign
+        came = me - sign * distance
+        sends = (owner >= 0) & (owner < n_dir) & (target >= 0) & (target < n_dir)
+        where = all_ref.at[pl.ds(owner * pairs + chunk * part, part)]
+        copy = pltpu.make_async_remote_copy(
+            src_ref=where, dst_ref=where, send_sem=send_sem.at[side, distance, chunk],
+            recv_sem=recv_sem.at[side, distance, chunk],
+            device_id={"dir": target}, device_id_type=pl.DeviceIdType.MESH)
+        there = all_ref.at[pl.ds(came * pairs + chunk * part, part)]
+        arrival = pltpu.make_async_remote_copy(
+            src_ref=there, dst_ref=there, send_sem=send_sem.at[side, distance, chunk],
+            recv_sem=recv_sem.at[side, distance, chunk],
+            device_id={"dir": target}, device_id_type=pl.DeviceIdType.MESH)
+        return copy, sends, arrival, (came >= 0) & (came < n_dir)
+
+    def launch(distance, side, chunk):
+        @pl.when(hop(side, distance, chunk)[1])
+        def _():
+            hop(side, distance, chunk)[0].start()
+
+    lanes_of = [(chunk, side) for chunk in range(CHUNKS) for side in range(2)]
+    for chunk, side in lanes_of:
+        launch(1, side, chunk)
     @pl.when(jnp.logical_not(has_before))
     def _():
         before_ref[...] = jnp.zeros_like(before_ref)
@@ -66,8 +83,30 @@
     def _():
         after_ref[...] = jnp.zeros_like(after_ref)
 
-    for copy in copies[: n_dir - 1]:
-        copy.wait_recv()
+    for distance in range(1, n_dir):
+        for chunk, side in lanes_of:
+            @pl.when(hop(side, distance, chunk)[3])
+            def _(side=side, distance=distance, chunk=chunk):
+                hop(side, distance, chunk)[2].wait_recv()
+
+            if distance < n_dir - 1:
+                launch(distance + 1, side, chunk)
+
+    core = lax.rem(cluster, 2)
+    half = rows // 2
+    tables, relays = [], []
+    for step in range(1, n_dir):
+        mine = kinds_ref.at[pl.ds(pl.multiple_of(me * rows + core * half, half), half)]
+        tables.append(pltpu.make_async_remote_copy(
+            src_ref=mine, dst_ref=mine, send_sem=tsend_sem.at[0, step], recv_sem=trecv_sem.at[0, step],
+            device_id={"dir": lax.rem(me + step, n_dir)}, device_id_type=pl.DeviceIdType.MESH))
+        owner = lax.rem(me + n_dir - step, n_dir)
+        got = kinds_ref.at[pl.ds(pl.multiple_of(owner * rows + core * half, half), half)]
+        relays.append(pltpu.make_async_remote_copy(
+            src_ref=got, dst_ref=got, send_sem=tsend_sem.at[1, step], recv_sem=trecv_sem.at[1, step],
+            device_id={"clus": cluster + 1 - 2 * core}, device_id_type=pl.DeviceIdType.MESH))
+    for copy in tables:
+        copy.start()
     width = units_ref.shape[2] // 2
 
     def pick(row, m):
@@ -93,10 +132,18 @@
         def _(copy=copy):
             copy.start()
 
-    for copy in copies[n_dir - 1 :]:
+    for copy, relay in zip(tables, relays):
         copy.wait_recv()
-    for copy in copies:
+        relay.start()
+    for copy in relays:
+        copy.wait_recv()
+    for copy in tables + relays:
         copy.wait_send()
+    for distance in range(1, n_dir):
+        for chunk, side in lanes_of:
+            @pl.when(hop(side, distance, chunk)[1])
+            def _(side=side, distance=distance, chunk=chunk):
+                hop(side, distance, chunk)[0].wait_send()
 
     @pl.when(has_after)
     def _():
@@ -247,7 +294,8 @@
         in_specs=[pl.BlockSpec(memory_space=SMEM)] * 2 + [pl.BlockSpec(memory_space=VMEM)] * 2,
         out_specs=[pl.BlockSpec(memory_space=VMEM)] * 4,
         scratch_shapes=[VMEM(sent, BF16), VMEM(sent, BF16)]
-        + [pltpu.SemaphoreType.DMA((n_dir,))] * 4
+        + [pltpu.SemaphoreType.DMA((2, n_dir, CHUNKS))] * 2
+        + [pltpu.SemaphoreType.DMA((2, n_dir))] * 2
         + [pltpu.SemaphoreType.DMA((2,))] * 2,
         compiler_params=pltpu.CompilerParams(
             collective_id=0, has_side_effects=True, vmem_limit_bytes=32 * 2**20

time: 67.9 us -> 62.9 us (0.926)
  the two profiles are of different devices: /device:TPU:9 before, /device:TPU:1 now
where the time goes in v4:
time: 62.9 us; the launch traced here: 62.6 us
  Pallas kernels  51.2 us (81%)
  local copies, waits for them, and re-layouts  9.98 us (16%)
  other arithmetic  1.37 us (2%)
    pallas_call x1, Pallas kernels, per_device(): pl.pallas_call(functools.partial(exchange, n_dir, n_clus), out_shape=[jax...  33.7 us
    pallas_call x1, Pallas kernels, per_device(): pl.pallas_call(compute, grid=(steps,), out_shape=jax.ShapeDtypeStruct((un...  17.5 us
    unnamed x15, local copies, waits for them, and re-layouts  7.16 us
    dynamic_slice x1, local copies, waits for them, and re-layouts, per_device(): own_count = lax.dynamic_slice_in_dim(live_counts[0], dir_index, 1, 0)  1.33 us
    dynamic_slice x1, local copies, waits for them, and re-layouts, per_device(): lax.dynamic_slice_in_dim(far_translators, dir_index * capacity, capacity, 0)  1.32 us

profile of v4, /device:TPU:1, one launch (start us, length us, event | category | flops | bytes accessed | tf_op | source)
XLA Modules:
  0.0 62.6 jit_solution(5577356657551925173)
XLA Ops:
  0.0 0.0 copy-start
  0.0 1.3 %constant_dynamic-slice_fusion.2 = s32[1,1]{1,0:T(1,128)} fusion(s32[1,4]{1,0:T(1,128)} %param.10, s32[]{:T(128)S(6)} %select_n.19), kind=kLoop, calls=%fused_computation.13 | loop fusion | bytes 12 | tf_op jit(solution)/shard_map/dynamic_slice | solution.py:279
  1.3 0.6 %fusion.1 = bf16[8,2]{1,0:T(8,128)(2,1)S(1)} fusion(s32[]{:T(128)} %bitcast.2), kind=kLoop, calls=%fused_computation.3 | loop fusion | flops 64 | bytes 36 | tf_op jit(solution)/shard_map/convert_element_type | solution.py:281
  2.0 0.1 mul.17
  2.0 0.1 mul.18
  2.1 0.7 %and_select_fusion = (s32[2,32]{1,0:T(2,128)S(1)}, s32[2,32]{1,0:T(2,128)S(1)}) fusion(s32[1,2,32]{2,1,0:T(2,128)} %param.13), kind=kLoop, calls=%fused_computation.4 | loop fusion | flops 1216 | bytes 768 | tf_op jit(solution)/shard_map/jit(remainder)/select_n | solution.py:304
  2.8 1.4 %copy.15.near_cols_ref = s32[16,6]{1,0:T(8,128)} copy(s32[16,6]{0,1:T(8,128)} %param.17) | data formatting | bytes 768 | tf_op args[8]
  4.2 1.3 %constant_dynamic-slice_fusion = (s32[16,128]{1,0:T(8,128)}, s32[16,128]{1,0:T(8,128)}) fusion(s32[64,128]{1,0:T(8,128)} %param.15, s32[]{:T(128)S(6)} %select_n.22, s32[64,128]{1,0:T(8,128)} %param.14), kind=kLoop, calls=%fused_computation.11 | loop fusion | bytes 32772 | tf_op jit(solution)/shard_map/dynamic_slice | solution.py:306
  5.5 1.0 %copy.14 = bf16[316,128]{0,1:T(8,128)(2,1)S(1)} copy(bf16[316,128]{1,0:T(8,128)(2,1)} %param.12) | data formatting | bytes 161792 | tf_op args[3]
  6.5 1.6 %copy.16.agg_ref = bf16[512,96]{1,0:T(8,128)(2,1)} copy(bf16[512,96]{0,1:T(8,128)(2,1)} %param.11) | data formatting | bytes 196608 | tf_op args[2]
  8.2 0.0 copy-done
  8.2 0.0 copy-start.1
  8.2 33.7 %exchange.1 = (bf16[32,96,128]{2,1,0:T(8,128)(2,1)S(1)}, bf16[16,96,128]{2,1,0:T(8,128)(2,1)S(1)}, bf16[16,96,128]{2,1,0:T(8,128)(2,1)S(1)}, bf16[512,384]{1,0:T(8,128)(2,1)S(1)}) custom-call(s32[2,32]{1,0:T(2,128)S(1)} %get-tuple-element.14.pair_ref, s32[2,32]{1,0:T(2,128)S(1)} %get-tuple-element.13.half_ref, bf16[8,96,128]{2,1,0:T(8,128)(2,1)S(1)} %fusion.units_ref, ...), custom_call_target="tpu_custom_call" | custom-call | tf_op jit(solution)/shard_map/exchange/pallas_call | solution.py:286
  41.9 0.0 copy-start.2
  41.9 0.9 %copy-done.2 = bf16[32,96,128]{2,1,0:T(8,128)(2,1)} copy-done((bf16[32,96,128]{2,1,0:T(8,128)(2,1)}, bf16[32,96,128]{2,1,0:T(8,128)(2,1)S(1)}, u32[]{:S(2)}) %copy-start.2) | copy-done | bytes 786456
  42.8 0.0 copy-start.3
  42.8 0.8 %copy-done.3 = bf16[16,96,128]{2,1,0:T(8,128)(2,1)} copy-done((bf16[16,96,128]{2,1,0:T(8,128)(2,1)}, bf16[16,96,128]{2,1,0:T(8,128)(2,1)S(1)}, u32[]{:S(2)}) %copy-start.3) | copy-done | bytes 393240
  43.5 0.0 copy-start.4
  43.5 0.8 %copy-done.4 = bf16[16,96,128]{2,1,0:T(8,128)(2,1)} copy-done((bf16[16,96,128]{2,1,0:T(8,128)(2,1)}, bf16[16,96,128]{2,1,0:T(8,128)(2,1)S(1)}, u32[]{:S(2)}) %copy-start.4) | copy-done | bytes 393240
  44.3 0.0 copy-start.5
  44.3 0.7 %copy-done.5 = bf16[512,384]{1,0:T(8,128)(2,1)} copy-done((bf16[512,384]{1,0:T(8,128)(2,1)}, bf16[512,384]{1,0:T(8,128)(2,1)S(1)}, u32[]{:S(2)}) %copy-start.5) | copy-done | bytes 393240
  45.0 0.0 copy-done.1
  45.0 17.5 %compute.1 = bf16[96,1024]{1,0:T(8,128)(2,1)} custom-call(s32[1]{0:T(128)} %bitcast.count_ref, s32[16,6]{1,0:T(8,128)} %copy.15.near_cols_ref, bf16[32,96,128]{2,1,0:T(8,128)(2,1)} %copy-done.2, bf16[16,96,128]{2,1,0:T(8,128)(2,1)} %copy-done.3, bf16[16,96,128]{2,1,0:T(8,128)(2,1)} %copy-done.4, bf16[512,384]{1,0:T(8,128)(2,1)} %copy-done.5, ...), custom_call_target="tpu_custom_call" | custom-call | tf_op jit(solution)/shard_map/compute/pallas_call | solution.py:311
  (2 shorter events, 0.1 us)
Async XLA Ops:
  0.0 8.2 %copy-start = (bf16[96,1024]{1,0:T(8,128)(2,1)S(1)}, bf16[96,1024]{1,0:T(8,128)(2,1)}, u32[]{:S(2)}) copy-start(bf16[96,1024]{1,0:T(8,128)(2,1)} %param.9) | copy-start | bytes 589828
  8.2 36.8 %copy-start.1 = (bf16[8,96,128]{2,1,0:T(8,128)(2,1)}, bf16[8,96,128]{2,1,0:T(8,128)(2,1)S(1)}, u32[]{:S(2)}) copy-start(bf16[8,96,128]{2,1,0:T(8,128)(2,1)S(1)} %fusion.units_ref) | copy-start | bytes 589828
  41.9 0.9 %copy-start.2 = (bf16[32,96,128]{2,1,0:T(8,128)(2,1)}, bf16[32,96,128]{2,1,0:T(8,128)(2,1)S(1)}, u32[]{:S(2)}) copy-start(bf16[32,96,128]{2,1,0:T(8,128)(2,1)S(1)} %get-tuple-element.9.all_ref) | copy-start | bytes 2359300
  42.8 0.8 %copy-start.3 = (bf16[16,96,128]{2,1,0:T(8,128)(2,1)}, bf16[16,96,128]{2,1,0:T(8,128)(2,1)S(1)}, u32[]{:S(2)}) copy-start(bf16[16,96,128]{2,1,0:T(8,128)(2,1)S(1)} %get-tuple-element.10.before_ref) | copy-start | bytes 1179652
  43.5 0.8 %copy-start.4 = (bf16[16,96,128]{2,1,0:T(8,128)(2,1)}, bf16[16,96,128]{2,1,0:T(8,128)(2,1)S(1)}, u32[]{:S(2)}) copy-start(bf16[16,96,128]{2,1,0:T(8,128)(2,1)S(1)} %get-tuple-element.11.after_ref) | copy-start | bytes 1179652
  44.3 0.8 %copy-start.5 = (bf16[512,384]{1,0:T(8,128)(2,1)}, bf16[512,384]{1,0:T(8,128)(2,1)S(1)}, u32[]{:S(2)}) copy-start(bf16[512,384]{1,0:T(8,128)(2,1)S(1)} %get-tuple-element.12.kinds_ref) | copy-start | bytes 1179652

commit v5 on v4

--- a/solution.py
+++ b/solution.py
@@ -8,7 +8,7 @@
 from jax.sharding import PartitionSpec as P
 
 LANES = 128
-CHUNKS = 2
+CHUNKS = 4
 GAP = 8
 SCRATCH_BYTES = 32 * 2**20
 F32 = jnp.float32
@@ -126,7 +126,7 @@
             ref[p] = jnp.concatenate([pick(row, 2 * p), pick(row, 2 * p + 1)], axis=1)
             return carry
 
-        lax.fori_loop(0, ref.shape[0], fill, 0)
+        lax.fori_loop(0, ref.shape[0], fill, 0, unroll=4)
 
         @pl.when(there)
         def _(copy=copy):
@@ -211,7 +211,7 @@
                 w_ref[c, pl.ds(at, block), : hi - lo] = made[:, half * pairs + lo : half * pairs + hi]
         return carry
 
-    lax.fori_loop(0, capacity, weigh, 0, unroll=8)
+    lax.fori_loop(0, capacity, weigh, 0, unroll=16)
 
     def translate(k, carry):
         e = e_ref[pl.ds(k, pairs, stride=stride), :].astype(BF16)

time: 62.9 us -> 59.8 us (0.951)
  Pallas kernels: 51.2 us -> 48.1 us
    pallas_call x1, Pallas kernels: 33.7 us -> 31.1 us  [per_device(): pl.pallas_call(functools.partial(exchange, n_dir, n_clus), out_shape=[jax...]
where the time goes in v5:
time: 59.8 us; the launch traced here: 59.5 us
  Pallas kernels  48.1 us (80%)
  local copies, waits for them, and re-layouts  9.98 us (17%)
  other arithmetic  1.37 us (2%)
    pallas_call x1, Pallas kernels, per_device(): pl.pallas_call(functools.partial(exchange, n_dir, n_clus), out_shape=[jax...  31.1 us
    pallas_call x1, Pallas kernels, per_device(): pl.pallas_call(compute, grid=(steps,), out_shape=jax.ShapeDtypeStruct((un...  17 us
    unnamed x15, local copies, waits for them, and re-layouts  7.16 us
    dynamic_slice x1, local copies, waits for them, and re-layouts, per_device(): own_count = lax.dynamic_slice_in_dim(live_counts[0], dir_index, 1, 0)  1.33 us
    dynamic_slice x1, local copies, waits for them, and re-layouts, per_device(): lax.dynamic_slice_in_dim(far_translators, dir_index * capacity, capacity, 0)  1.32 us

profile of v5, /device:TPU:1, one launch (start us, length us, event | category | flops | bytes accessed | tf_op | source)
XLA Modules:
  0.0 59.5 jit_solution(12759354391042475958)
XLA Ops:
  0.0 0.0 copy-start
  0.0 1.3 %constant_dynamic-slice_fusion.2 = s32[1,1]{1,0:T(1,128)} fusion(s32[1,4]{1,0:T(1,128)} %param.10, s32[]{:T(128)S(6)} %select_n.19), kind=kLoop, calls=%fused_computation.13 | loop fusion | bytes 12 | tf_op jit(solution)/shard_map/dynamic_slice | solution.py:279
  1.3 0.6 %fusion.1 = bf16[8,2]{1,0:T(8,128)(2,1)S(1)} fusion(s32[]{:T(128)} %bitcast.2), kind=kLoop, calls=%fused_computation.3 | loop fusion | flops 64 | bytes 36 | tf_op jit(solution)/shard_map/convert_element_type | solution.py:281
  2.0 0.1 mul.17
  2.0 0.1 mul.18
  2.1 0.7 %and_select_fusion = (s32[2,32]{1,0:T(2,128)S(1)}, s32[2,32]{1,0:T(2,128)S(1)}) fusion(s32[1,2,32]{2,1,0:T(2,128)} %param.13), kind=kLoop, calls=%fused_computation.4 | loop fusion | flops 1216 | bytes 768 | tf_op jit(solution)/shard_map/jit(remainder)/select_n | solution.py:304
  2.8 1.4 %copy.15.near_cols_ref = s32[16,6]{1,0:T(8,128)} copy(s32[16,6]{0,1:T(8,128)} %param.17) | data formatting | bytes 768 | tf_op args[8]
  4.2 1.3 %constant_dynamic-slice_fusion = (s32[16,128]{1,0:T(8,128)}, s32[16,128]{1,0:T(8,128)}) fusion(s32[64,128]{1,0:T(8,128)} %param.15, s32[]{:T(128)S(6)} %select_n.22, s32[64,128]{1,0:T(8,128)} %param.14), kind=kLoop, calls=%fused_computation.11 | loop fusion | bytes 32772 | tf_op jit(solution)/shard_map/dynamic_slice | solution.py:306
  5.5 1.0 %copy.14 = bf16[316,128]{0,1:T(8,128)(2,1)S(1)} copy(bf16[316,128]{1,0:T(8,128)(2,1)} %param.12) | data formatting | bytes 161792 | tf_op args[3]
  6.5 1.6 %copy.16.agg_ref = bf16[512,96]{1,0:T(8,128)(2,1)} copy(bf16[512,96]{0,1:T(8,128)(2,1)} %param.11) | data formatting | bytes 196608 | tf_op args[2]
  8.2 0.0 copy-done
  8.2 0.0 copy-start.1
  8.2 31.1 %exchange.1 = (bf16[32,96,128]{2,1,0:T(8,128)(2,1)S(1)}, bf16[16,96,128]{2,1,0:T(8,128)(2,1)S(1)}, bf16[16,96,128]{2,1,0:T(8,128)(2,1)S(1)}, bf16[512,384]{1,0:T(8,128)(2,1)S(1)}) custom-call(s32[2,32]{1,0:T(2,128)S(1)} %get-tuple-element.14.pair_ref, s32[2,32]{1,0:T(2,128)S(1)} %get-tuple-element.13.half_ref, bf16[8,96,128]{2,1,0:T(8,128)(2,1)S(1)} %fusion.units_ref, ...), custom_call_target="tpu_custom_call" | custom-call | tf_op jit(solution)/shard_map/exchange/pallas_call | solution.py:286
  39.3 0.0 copy-start.2
  39.3 0.9 %copy-done.2 = bf16[32,96,128]{2,1,0:T(8,128)(2,1)} copy-done((bf16[32,96,128]{2,1,0:T(8,128)(2,1)}, bf16[32,96,128]{2,1,0:T(8,128)(2,1)S(1)}, u32[]{:S(2)}) %copy-start.2) | copy-done | bytes 786456
  40.2 0.0 copy-start.3
  40.2 0.8 %copy-done.3 = bf16[16,96,128]{2,1,0:T(8,128)(2,1)} copy-done((bf16[16,96,128]{2,1,0:T(8,128)(2,1)}, bf16[16,96,128]{2,1,0:T(8,128)(2,1)S(1)}, u32[]{:S(2)}) %copy-start.3) | copy-done | bytes 393240
  41.0 0.0 copy-start.4
  41.0 0.8 %copy-done.4 = bf16[16,96,128]{2,1,0:T(8,128)(2,1)} copy-done((bf16[16,96,128]{2,1,0:T(8,128)(2,1)}, bf16[16,96,128]{2,1,0:T(8,128)(2,1)S(1)}, u32[]{:S(2)}) %copy-start.4) | copy-done | bytes 393240
  41.7 0.0 copy-start.5
  41.7 0.7 %copy-done.5 = bf16[512,384]{1,0:T(8,128)(2,1)} copy-done((bf16[512,384]{1,0:T(8,128)(2,1)}, bf16[512,384]{1,0:T(8,128)(2,1)S(1)}, u32[]{:S(2)}) %copy-start.5) | copy-done | bytes 393240
  42.5 0.0 copy-done.1
  42.5 17.0 %compute.1 = bf16[96,1024]{1,0:T(8,128)(2,1)} custom-call(s32[1]{0:T(128)} %bitcast.count_ref, s32[16,6]{1,0:T(8,128)} %copy.15.near_cols_ref, bf16[32,96,128]{2,1,0:T(8,128)(2,1)} %copy-done.2, bf16[16,96,128]{2,1,0:T(8,128)(2,1)} %copy-done.3, bf16[16,96,128]{2,1,0:T(8,128)(2,1)} %copy-done.4, bf16[512,384]{1,0:T(8,128)(2,1)} %copy-done.5, ...), custom_call_target="tpu_custom_call" | custom-call | tf_op jit(solution)/shard_map/compute/pallas_call | solution.py:311
  (2 shorter events, 0.1 us)
Async XLA Ops:
  0.0 8.2 %copy-start = (bf16[96,1024]{1,0:T(8,128)(2,1)S(1)}, bf16[96,1024]{1,0:T(8,128)(2,1)}, u32[]{:S(2)}) copy-start(bf16[96,1024]{1,0:T(8,128)(2,1)} %param.9) | copy-start | bytes 589828
  8.2 34.3 %copy-start.1 = (bf16[8,96,128]{2,1,0:T(8,128)(2,1)}, bf16[8,96,128]{2,1,0:T(8,128)(2,1)S(1)}, u32[]{:S(2)}) copy-start(bf16[8,96,128]{2,1,0:T(8,128)(2,1)S(1)} %fusion.units_ref) | copy-start | bytes 589828
  39.3 0.9 %copy-start.2 = (bf16[32,96,128]{2,1,0:T(8,128)(2,1)}, bf16[32,96,128]{2,1,0:T(8,128)(2,1)S(1)}, u32[]{:S(2)}) copy-start(bf16[32,96,128]{2,1,0:T(8,128)(2,1)S(1)} %get-tuple-element.9.all_ref) | copy-start | bytes 2359300
  40.2 0.8 %copy-start.3 = (bf16[16,96,128]{2,1,0:T(8,128)(2,1)}, bf16[16,96,128]{2,1,0:T(8,128)(2,1)S(1)}, u32[]{:S(2)}) copy-start(bf16[16,96,128]{2,1,0:T(8,128)(2,1)S(1)} %get-tuple-element.10.before_ref) | copy-start | bytes 1179652
  41.0 0.8 %copy-start.4 = (bf16[16,96,128]{2,1,0:T(8,128)(2,1)}, bf16[16,96,128]{2,1,0:T(8,128)(2,1)S(1)}, u32[]{:S(2)}) copy-start(bf16[16,96,128]{2,1,0:T(8,128)(2,1)S(1)} %get-tuple-element.11.after_ref) | copy-start | bytes 1179652
  41.7 0.8 %copy-start.5 = (bf16[512,384]{1,0:T(8,128)(2,1)}, bf16[512,384]{1,0:T(8,128)(2,1)S(1)}, u32[]{:S(2)}) copy-start(bf16[512,384]{1,0:T(8,128)(2,1)S(1)} %get-tuple-element.12.kinds_ref) | copy-start | bytes 1179652
